TPU v7x, 256 devices: a whole 4x4x8 slice. The times are simulated.
256 devices in a mesh: lat: 16 (over x_hi, y, core), lon: 16 (over x_lo, z).
Axes of the slice: x: 4 (x_hi: 2, x_lo: 2; x = x_hi * 2 + x_lo), y: 4, z: 8, core: 2. Of those that a mesh axis runs over, the one named last changes fastest.
Arguments:
- series: bfloat16 [16, 16, 3, 64, 128, 128], P('lat', 'lon')
- station_count: int32 [16, 16], P('lat', 'lon'), may hold values from 32 to 128, as said below
- pair_count: int32 [16, 16], P('lat', 'lon'), may hold values from 64 to 256, as said below
- pair_list: int32 [16, 16, 3, 256], P('lat', 'lon'), may hold values from 0 to 8, as said below
- band_bins: int32 [16], replicated, may hold values from 1 to 63, as said below
Outputs:
- tensors: float32 [16, 16, 256, 12, 256], P('lat', 'lon')
Inputs may be any that keep to these rules, and one draw needn't show every extreme that they name: `station_count`: slots below a tile's count hold live stations; some tile is full in every draw. `pair_count`: some tile's list is full in every draw; entries at and beyond a tile's count are ignored. `pair_list`: row 0 holds offset codes 0 to 8, rows 1 and 2 block numbers below 8. `band_bins`: 16 distinct bins; the lowest and the highest allowed bin are always among them.
All inputs are finite; a program needn't handle non-finite values.
Results may differ from a plain program's by a relative error of at most 0.00032.
Values may be sent and summed in bfloat16 or wider, within the bound.
A program may use at most 256 MiB of HBM per device.

v0:
```python
import math

import jax
import jax.numpy as jnp
from jax import lax
from jax.sharding import PartitionSpec as P

BLOCK = 16


def with_halo(array, sides, width):
    for axis, dim in sides:
        devices, length = (lax.axis_size(axis), array.shape[dim])
        up = [(i, (i + 1) % devices) for i in range(devices - 1)]
        down = [(j, i) for i, j in up]
        last = lax.slice_in_dim(array, length - width, length, axis=dim)
        initial = lax.slice_in_dim(array, 0, width, axis=dim)
        before = lax.ppermute(last, axis, up)
        after = lax.ppermute(initial, axis, down)
        array = jnp.concatenate([before, array, after], axis=dim)
    return array


def dft_table(band_bins, length):
    samples = jnp.arange(length, dtype=jnp.int32)
    phase = band_bins[None, :] * samples[:, None] % length
    angle = phase.astype(jnp.float32) * (2.0 * math.pi / length)
    factor = 1.0 / math.sqrt(length)
    table = jnp.stack([jnp.cos(angle) * factor, -jnp.sin(angle) * factor], axis=1)
    return table.astype(jnp.bfloat16)


def gram_terms(nearby):
    real_x = nearby[:, 0, :, 0, :].astype(jnp.float32)
    imag_x = nearby[:, 0, :, 1, :].astype(jnp.float32)
    real_y = nearby[:, 1, :, 0, :].astype(jnp.float32)
    imag_y = nearby[:, 1, :, 1, :].astype(jnp.float32)
    gram_xx = jnp.sum(real_x * real_x + imag_x * imag_x, -1)
    gram_yy = jnp.sum(real_y * real_y + imag_y * imag_y, -1)
    gram_re = jnp.sum(real_x * real_y + imag_x * imag_y, -1)
    gram_im = jnp.sum(real_x * imag_y - imag_x * real_y, -1)
    return (gram_xx, gram_yy, gram_re, gram_im)


def solve_pair(cross_re, cross_im, gram_xx, gram_yy, gram_re, gram_im, ridge):
    upper_xx = gram_xx + ridge
    lower_yy = gram_yy + ridge
    determinant = upper_xx * lower_yy - (gram_re * gram_re + gram_im * gram_im)
    first_re, second_re = (cross_re[:, :, 0], cross_re[:, :, 1])
    first_im, second_im = (cross_im[:, :, 0], cross_im[:, :, 1])
    top_re = (lower_yy * first_re - (gram_re * second_re - gram_im * second_im)) / determinant
    top_im = (lower_yy * first_im - (gram_re * second_im + gram_im * second_re)) / determinant
    low_re = (upper_xx * second_re - (gram_re * first_re + gram_im * first_im)) / determinant
    low_im = (upper_xx * second_im - (gram_re * first_im - gram_im * first_re)) / determinant
    stacked = jnp.stack([jnp.stack([top_re, top_im], 1), jnp.stack([low_re, low_im], 1)], 0)
    block = stacked.shape[3]
    return stacked.reshape(12, block * block)


def per_device(series, station_count, pair_count, pair_list, band_bins):
    table = dft_table(band_bins, series.shape[-1])
    spectra = jnp.einsum("cwsn,nrk->csrkw", series[0, 0], table, preferred_element_type=jnp.float32)
    comps, slots = (spectra.shape[0], spectra.shape[1])
    spectra = spectra.reshape(comps, slots, 2, -1)
    live = (jnp.arange(slots, dtype=jnp.int32) < station_count[0, 0]).astype(jnp.float32)
    spectra = (spectra * live[None, :, None, None]).astype(jnp.bfloat16)
    horizontal = spectra[:2]
    widened = horizontal.astype(jnp.float32)
    power = 0.5 * jnp.sum(widened * widened)
    total_power, total_count = lax.psum(
        (power, station_count[0, 0].astype(jnp.float32)), ("lat", "lon")
    )
    ridge = total_power / total_count + 1e-06
    framed = horizontal[None, None]
    nearby = with_halo(framed, (("lat", 0), ("lon", 1)), 1)
    width = spectra.shape[-1]
    nearby = nearby.reshape(9, 2, slots, 2, width)
    block = BLOCK
    blocks = slots // block
    gram_xx, gram_yy, gram_re, gram_im = gram_terms(nearby)
    gram_xx = gram_xx.reshape(9, blocks, block)
    gram_yy = gram_yy.reshape(9, blocks, block)
    gram_re = gram_re.reshape(9, blocks, block)
    gram_im = gram_im.reshape(9, blocks, block)
    listing = pair_list[0, 0]
    pairs = listing.shape[1]
    batched_solve = jax.vmap(solve_pair, in_axes=(0, 0, 0, 0, 0, 0, None))
    target_view = spectra.reshape(comps, blocks, block, 2, width)
    near_view = nearby.reshape(9, 2, blocks, block, 2, width)
    group = min(64, pairs)
    while pairs % group != 0:
        group = group // 2

    def one_group(chosen):
        offsets, local_blocks, near_index = (chosen[0], chosen[1], chosen[2])
        targets = target_view[:, local_blocks]
        partners = near_view[offsets, :, near_index]
        cross_re = jnp.einsum(
            "tpim,pajm->ptiaj",
            targets[:, :, :, 0],
            partners[:, :, :, 0],
            preferred_element_type=jnp.float32,
        ) + jnp.einsum(
            "tpim,pajm->ptiaj",
            targets[:, :, :, 1],
            partners[:, :, :, 1],
            preferred_element_type=jnp.float32,
        )
        cross_im = jnp.einsum(
            "tpim,pajm->ptiaj",
            targets[:, :, :, 1],
            partners[:, :, :, 0],
            preferred_element_type=jnp.float32,
        ) - jnp.einsum(
            "tpim,pajm->ptiaj",
            targets[:, :, :, 0],
            partners[:, :, :, 1],
            preferred_element_type=jnp.float32,
        )
        return batched_solve(
            cross_re,
            cross_im,
            gram_xx[offsets, near_index],
            gram_yy[offsets, near_index],
            gram_re[offsets, near_index],
            gram_im[offsets, near_index],
            ridge,
        )

    batches = listing.reshape(3, pairs // group, group).transpose(1, 0, 2)
    solved = lax.map(one_group, batches).reshape(pairs, 12, block * block)
    keep = (jnp.arange(pairs, dtype=jnp.int32) < pair_count[0, 0]).astype(jnp.float32)
    return (solved * keep[:, None, None])[None, None]


def solution(mesh):
    in_specs = (
        P("lat", "lon", None, None, None, None),
        P("lat", "lon"),
        P("lat", "lon"),
        P("lat", "lon", None, None),
        P(),
    )
    out_specs = P("lat", "lon", None, None, None)
    return jax.shard_map(
        per_device, mesh=mesh, in_specs=in_specs, out_specs=out_specs, check_vma=False
    )
```

profile of v0, /device:TPU:4, one launch (start us, length us, event | category | flops | bytes accessed | tf_op | source)
XLA Modules:
  0.0 629.8 jit_solution(14080607036713378395)
XLA Ops:
  1.5 5.0 fusion.19
  8.6 4.3 collective-permute-start.1
  14.9 10.4 %collective-permute-done.1 = bf16[1,1,2,128,2,1024]{3,5,4,2,1,0:T(8,128)(2,1)S(1)} collective-permute-done((bf16[1,1,2,128,2,1024]{3,5,4,2,1,0:T(8,128)(2,1)S(1)}, bf16[1,1,2,128,2,1024]{3,5,4,2,1,0:T(8,128)(2,1)S(1)}, u32[]{:S(2)}, u32[]{:S(2)}) %collective-permute-start.1) | collective-permute-done | bytes 1048608 | tf_op jit(solution)/shard_map/ppermute | solution.py:19
  25.2 7.4 %collective-permute-done = bf16[1,1,2,128,2,1024]{3,5,4,2,1,0:T(8,128)(2,1)S(1)} collective-permute-done((bf16[1,1,2,128,2,1024]{3,5,4,2,1,0:T(8,128)(2,1)S(1)}, bf16[1,1,2,128,2,1024]{3,5,4,2,1,0:T(8,128)(2,1)S(1)}, u32[]{:S(2)}, u32[]{:S(2)}) %collective-permute-start) | collective-permute-done | bytes 1048608 | tf_op jit(solution)/shard_map/ppermute | solution.py:18
  33.6 2.0 pad_maximum_fusion.2
  37.0 6.2 collective-permute-start.2
  43.9 133.5 %all-reduce = (f32[]{:T(128)}, f32[]{:T(128)}) all-reduce(f32[]{:T(128)S(6)} %mul_shard_map.3, f32[]{:T(128)S(6)} %convert_element_type.66), channel_id=1, replica_groups=mesh['lat'=16,'lon'=16] {'lat','lon'}, use_global_device_ids=true, to_apply=%region_5.6 | all-reduce | flops 2 | bytes 16 | tf_op jit(solution)/shard_map/psum | solution.py:70
  177.3 6.4 %copy.72 = f32[3,128,2,16,64]{4,3,1,2,0:T(8,128)} copy(f32[3,128,2,16,64]{1,3,4,0,2:T(8,128)} %copy-done) | data formatting | bytes 6291456 | tf_op jit(solution)/shard_map/cwsn,nrk->csrkw/transpose | solution.py:62
  183.9 6.3 %reshape.436 = f32[3,8,16,2,1024]{4,2,1,3,0:T(8,128)} reshape(f32[3,128,2,16,64]{4,3,1,2,0:T(8,128)} %copy.72) | data formatting | bytes 6291456 | tf_op jit(solution)/shard_map/reshape | solution.py:64
  190.2 2.4 multiply_convert_fusion
  195.1 8.8 %pad_maximum_fusion.1 = bf16[3,3,2,128,2,1024]{3,5,4,2,1,0:T(8,128)(2,1)} fusion(bf16[3,1,2,128,2,1024]{3,5,4,2,1,0:T(8,128)(2,1)} %collective-permute-done.3, bf16[1,1,2,128,2,1024]{3,5,4,2,1,0:T(8,128)(2,1)} %copy-done.1, bf16[1,1,2,128,2,1024]{3,5,4,2,1,0:T(8,128)(2,1)S(1)} %get-tuple-element.138, bf16[1,1,2,128,2,1024]{3,5,4,2,1,0:T(8,128)(2,1)} %copy-done.2, ...), kind=kLoop, calls=%fused_computation.42 | loop fusion | flops 18874368 | bytes 18874368 | tf_op jit(solution)/shard_map/concatenate | solution.py:20
  203.9 12.7 %copy.73 = bf16[3,3,2,128,2,1024]{5,3,4,2,1,0:T(8,128)(2,1)} copy(bf16[3,3,2,128,2,1024]{3,5,4,2,1,0:T(8,128)(2,1)} %pad_maximum_fusion.1) | data formatting | bytes 18874368 | tf_op jit(solution)/shard_map/concatenate | solution.py:20
  216.6 5.5 fusion.17
  222.1 9.4 %copy.76 = bf16[9,2,8,16,2,1024]{5,3,4,2,1,0:T(8,128)(2,1)} copy(bf16[9,2,8,16,2,1024]{5,3,2,4,1,0:T(8,128)(2,1)} %bitcast.185) | data formatting | bytes 18874368 | tf_op jit(solution)/shard_map/while | solution.py:131
  231.8 394.0 %while.10 = (s32[]{:T(128)}, f32[4,64,12,256]{3,1,0,2:T(8,128)}, s32[4,3,64]{2,0,1:T(4,128)S(1)}, f32[9,8,16]{2,1,0:T(8,128)S(1)}, f32[]{:T(128)}, /*index=5*/bf...) while((s32[]{:T(128)}, f32[4,64,12,256]{3,1,0,2:T(8,128)}, ...), condition=%wide.region_8.9_spmd, body=%wide.region_7.8_spmd.sunk | while | flops 807084928 | bytes 124125624 | solution.py:131
  232.1 7.2 %gather_fusion = bf16[64,3,16,2,1024]{4,2,3,1,0:T(8,128)(2,1)} fusion(bf16[3,8,16,2,1024]{4,2,3,1,0:T(8,128)(2,1)S(1)} %get-tuple-element.257, s32[1024]{0:T(1024)S(1)} %pad_clamp_fusion.2), kind=kCustom, calls=%fused_computation.1.clone.1 | custom fusion | bytes 25166080 | tf_op jit(solution)/shard_map/while/body/eval_jaxpr/gather | solution.py:96
  239.2 10.9 %copy.110 = bf16[64,3,16,2,1024]{4,2,1,0,3:T(8,128)(2,1)} copy(bf16[64,3,16,2,1024]{4,2,3,1,0:T(8,128)(2,1)} %gather_fusion) | data formatting | bytes 25165824 | tf_op jit(solution)/shard_map/while/body/eval_jaxpr/gather | solution.py:96
  250.1 9.5 %gather_fusion.1 = bf16[64,2,16,2,1024]{4,2,3,1,0:T(8,128)(2,1)} fusion(bf16[9,2,8,16,2,1024]{5,3,4,2,1,0:T(8,128)(2,1)} %get-tuple-element.258, s32[64]{0:T(128)S(1)} %get-tuple-element.214), kind=kCustom, calls=%fused_computation.2.clone.1 | custom fusion | bytes 16777728 | tf_op jit(solution)/shard_map/while/body/eval_jaxpr/gather | solution.py:97
  259.6 12.1 %fusion.37 = f32[64,3,16,2,16]{4,2,3,1,0:T(8,128)} fusion(bf16[3,64,16,2,1024]{4,2,0,1,3:T(8,128)(2,1)} %bitcast.179, bf16[64,2,16,2,1024]{4,2,3,1,0:T(8,128)(2,1)} %gather_fusion.1), kind=kOutput, calls=%fused_computation.10.clone.1 | convolution fusion | flops 201326592 | bytes 10878976 | tf_op jit(solution)/shard_map/while/body/eval_jaxpr/tpim,pajm->ptiaj/dot_general | solution.py:98
  271.6 2.6 copy.111
  274.2 12.1 %fusion.38 = f32[64,3,16,2,16]{4,2,3,1,0:T(8,128)} fusion(bf16[3,64,16,2,1024]{4,2,0,1,3:T(8,128)(2,1)} %bitcast.180, bf16[64,2,16,2,1024]{4,2,3,1,0:T(8,128)(2,1)} %gather_fusion.1), kind=kOutput, calls=%fused_computation.12.clone.1 | convolution fusion | flops 201326592 | bytes 10878976 | tf_op jit(solution)/shard_map/while/body/eval_jaxpr/tpim,pajm->ptiaj/dot_general | solution.py:103
  286.3 3.3 copy.112
  290.8 12.1 %fusion.39 = f32[64,3,16,2,16]{4,2,3,1,0:T(8,128)} fusion(bf16[3,64,16,2,1024]{4,2,0,1,3:T(8,128)(2,1)} %bitcast.181, bf16[64,2,16,2,1024]{4,2,3,1,0:T(8,128)(2,1)} %gather_fusion.1), kind=kOutput, calls=%fused_computation.11.clone.1 | convolution fusion | flops 201326592 | bytes 10878976 | tf_op jit(solution)/shard_map/while/body/eval_jaxpr/tpim,pajm->ptiaj/dot_general | solution.py:109
  302.9 3.3 copy.113
  306.2 12.1 %fusion.40 = f32[64,3,16,2,16]{4,2,3,1,0:T(8,128)} fusion(bf16[3,64,16,2,1024]{4,2,0,1,3:T(8,128)(2,1)} %bitcast.182, bf16[64,2,16,2,1024]{4,2,3,1,0:T(8,128)(2,1)} %gather_fusion.1), kind=kOutput, calls=%fused_computation.9.clone.1 | convolution fusion | flops 201326592 | bytes 10878976 | tf_op jit(solution)/shard_map/while/body/eval_jaxpr/tpim,pajm->ptiaj/dot_general | solution.py:114
  318.3 3.3 copy.114
  328.4 2.1 constant_dynamic-update-slice_fusion.2
  330.5 7.2 %gather_fusion = bf16[64,3,16,2,1024]{4,2,3,1,0:T(8,128)(2,1)} fusion(bf16[3,8,16,2,1024]{4,2,3,1,0:T(8,128)(2,1)S(1)} %get-tuple-element.257, s32[1024]{0:T(1024)S(1)} %pad_clamp_fusion.2), kind=kCustom, calls=%fused_computation.1.clone.1 | custom fusion | bytes 25166080 | tf_op jit(solution)/shard_map/while/body/eval_jaxpr/gather | solution.py:96
  337.7 10.9 %copy.110 = bf16[64,3,16,2,1024]{4,2,1,0,3:T(8,128)(2,1)} copy(bf16[64,3,16,2,1024]{4,2,3,1,0:T(8,128)(2,1)} %gather_fusion) | data formatting | bytes 25165824 | tf_op jit(solution)/shard_map/while/body/eval_jaxpr/gather | solution.py:96
  348.5 9.5 %gather_fusion.1 = bf16[64,2,16,2,1024]{4,2,3,1,0:T(8,128)(2,1)} fusion(bf16[9,2,8,16,2,1024]{5,3,4,2,1,0:T(8,128)(2,1)} %get-tuple-element.258, s32[64]{0:T(128)S(1)} %get-tuple-element.214), kind=kCustom, calls=%fused_computation.2.clone.1 | custom fusion | bytes 16777728 | tf_op jit(solution)/shard_map/while/body/eval_jaxpr/gather | solution.py:97
  358.0 12.1 %fusion.37 = f32[64,3,16,2,16]{4,2,3,1,0:T(8,128)} fusion(bf16[3,64,16,2,1024]{4,2,0,1,3:T(8,128)(2,1)} %bitcast.179, bf16[64,2,16,2,1024]{4,2,3,1,0:T(8,128)(2,1)} %gather_fusion.1), kind=kOutput, calls=%fused_computation.10.clone.1 | convolution fusion | flops 201326592 | bytes 10878976 | tf_op jit(solution)/shard_map/while/body/eval_jaxpr/tpim,pajm->ptiaj/dot_general | solution.py:98
  370.1 2.6 copy.111
  372.7 12.1 %fusion.38 = f32[64,3,16,2,16]{4,2,3,1,0:T(8,128)} fusion(bf16[3,64,16,2,1024]{4,2,0,1,3:T(8,128)(2,1)} %bitcast.180, bf16[64,2,16,2,1024]{4,2,3,1,0:T(8,128)(2,1)} %gather_fusion.1), kind=kOutput, calls=%fused_computation.12.clone.1 | convolution fusion | flops 201326592 | bytes 10878976 | tf_op jit(solution)/shard_map/while/body/eval_jaxpr/tpim,pajm->ptiaj/dot_general | solution.py:103
  384.8 3.3 copy.112
  389.3 12.1 %fusion.39 = f32[64,3,16,2,16]{4,2,3,1,0:T(8,128)} fusion(bf16[3,64,16,2,1024]{4,2,0,1,3:T(8,128)(2,1)} %bitcast.181, bf16[64,2,16,2,1024]{4,2,3,1,0:T(8,128)(2,1)} %gather_fusion.1), kind=kOutput, calls=%fused_computation.11.clone.1 | convolution fusion | flops 201326592 | bytes 10878976 | tf_op jit(solution)/shard_map/while/body/eval_jaxpr/tpim,pajm->ptiaj/dot_general | solution.py:109
  401.4 3.3 copy.113
  404.7 12.1 %fusion.40 = f32[64,3,16,2,16]{4,2,3,1,0:T(8,128)} fusion(bf16[3,64,16,2,1024]{4,2,0,1,3:T(8,128)(2,1)} %bitcast.182, bf16[64,2,16,2,1024]{4,2,3,1,0:T(8,128)(2,1)} %gather_fusion.1), kind=kOutput, calls=%fused_computation.9.clone.1 | convolution fusion | flops 201326592 | bytes 10878976 | tf_op jit(solution)/shard_map/while/body/eval_jaxpr/tpim,pajm->ptiaj/dot_general | solution.py:114
  416.8 3.3 copy.114
  426.9 2.1 constant_dynamic-update-slice_fusion.2
  429.0 7.2 %gather_fusion = bf16[64,3,16,2,1024]{4,2,3,1,0:T(8,128)(2,1)} fusion(bf16[3,8,16,2,1024]{4,2,3,1,0:T(8,128)(2,1)S(1)} %get-tuple-element.257, s32[1024]{0:T(1024)S(1)} %pad_clamp_fusion.2), kind=kCustom, calls=%fused_computation.1.clone.1 | custom fusion | bytes 25166080 | tf_op jit(solution)/shard_map/while/body/eval_jaxpr/gather | solution.py:96
  436.1 10.9 %copy.110 = bf16[64,3,16,2,1024]{4,2,1,0,3:T(8,128)(2,1)} copy(bf16[64,3,16,2,1024]{4,2,3,1,0:T(8,128)(2,1)} %gather_fusion) | data formatting | bytes 25165824 | tf_op jit(solution)/shard_map/while/body/eval_jaxpr/gather | solution.py:96
  447.0 9.5 %gather_fusion.1 = bf16[64,2,16,2,1024]{4,2,3,1,0:T(8,128)(2,1)} fusion(bf16[9,2,8,16,2,1024]{5,3,4,2,1,0:T(8,128)(2,1)} %get-tuple-element.258, s32[64]{0:T(128)S(1)} %get-tuple-element.214), kind=kCustom, calls=%fused_computation.2.clone.1 | custom fusion | bytes 16777728 | tf_op jit(solution)/shard_map/while/body/eval_jaxpr/gather | solution.py:97
  456.5 12.1 %fusion.37 = f32[64,3,16,2,16]{4,2,3,1,0:T(8,128)} fusion(bf16[3,64,16,2,1024]{4,2,0,1,3:T(8,128)(2,1)} %bitcast.179, bf16[64,2,16,2,1024]{4,2,3,1,0:T(8,128)(2,1)} %gather_fusion.1), kind=kOutput, calls=%fused_computation.10.clone.1 | convolution fusion | flops 201326592 | bytes 10878976 | tf_op jit(solution)/shard_map/while/body/eval_jaxpr/tpim,pajm->ptiaj/dot_general | solution.py:98
  468.6 2.6 copy.111
  471.1 12.1 %fusion.38 = f32[64,3,16,2,16]{4,2,3,1,0:T(8,128)} fusion(bf16[3,64,16,2,1024]{4,2,0,1,3:T(8,128)(2,1)} %bitcast.180, bf16[64,2,16,2,1024]{4,2,3,1,0:T(8,128)(2,1)} %gather_fusion.1), kind=kOutput, calls=%fused_computation.12.clone.1 | convolution fusion | flops 201326592 | bytes 10878976 | tf_op jit(solution)/shard_map/while/body/eval_jaxpr/tpim,pajm->ptiaj/dot_general | solution.py:103
  483.2 3.3 copy.112
  487.8 12.1 %fusion.39 = f32[64,3,16,2,16]{4,2,3,1,0:T(8,128)} fusion(bf16[3,64,16,2,1024]{4,2,0,1,3:T(8,128)(2,1)} %bitcast.181, bf16[64,2,16,2,1024]{4,2,3,1,0:T(8,128)(2,1)} %gather_fusion.1), kind=kOutput, calls=%fused_computation.11.clone.1 | convolution fusion | flops 201326592 | bytes 10878976 | tf_op jit(solution)/shard_map/while/body/eval_jaxpr/tpim,pajm->ptiaj/dot_general | solution.py:109
  499.9 3.3 copy.113
  503.1 12.1 %fusion.40 = f32[64,3,16,2,16]{4,2,3,1,0:T(8,128)} fusion(bf16[3,64,16,2,1024]{4,2,0,1,3:T(8,128)(2,1)} %bitcast.182, bf16[64,2,16,2,1024]{4,2,3,1,0:T(8,128)(2,1)} %gather_fusion.1), kind=kOutput, calls=%fused_computation.9.clone.1 | convolution fusion | flops 201326592 | bytes 10878976 | tf_op jit(solution)/shard_map/while/body/eval_jaxpr/tpim,pajm->ptiaj/dot_general | solution.py:114
  515.2 3.3 copy.114
  525.4 2.1 constant_dynamic-update-slice_fusion.2
  527.4 7.1 %gather_fusion = bf16[64,3,16,2,1024]{4,2,3,1,0:T(8,128)(2,1)} fusion(bf16[3,8,16,2,1024]{4,2,3,1,0:T(8,128)(2,1)S(1)} %get-tuple-element.257, s32[1024]{0:T(1024)S(1)} %pad_clamp_fusion.2), kind=kCustom, calls=%fused_computation.1.clone.1 | custom fusion | bytes 25166080 | tf_op jit(solution)/shard_map/while/body/eval_jaxpr/gather | solution.py:96
  534.6 10.9 %copy.110 = bf16[64,3,16,2,1024]{4,2,1,0,3:T(8,128)(2,1)} copy(bf16[64,3,16,2,1024]{4,2,3,1,0:T(8,128)(2,1)} %gather_fusion) | data formatting | bytes 25165824 | tf_op jit(solution)/shard_map/while/body/eval_jaxpr/gather | solution.py:96
  545.4 9.5 %gather_fusion.1 = bf16[64,2,16,2,1024]{4,2,3,1,0:T(8,128)(2,1)} fusion(bf16[9,2,8,16,2,1024]{5,3,4,2,1,0:T(8,128)(2,1)} %get-tuple-element.258, s32[64]{0:T(128)S(1)} %get-tuple-element.214), kind=kCustom, calls=%fused_computation.2.clone.1 | custom fusion | bytes 16777728 | tf_op jit(solution)/shard_map/while/body/eval_jaxpr/gather | solution.py:97
  554.9 12.1 %fusion.37 = f32[64,3,16,2,16]{4,2,3,1,0:T(8,128)} fusion(bf16[3,64,16,2,1024]{4,2,0,1,3:T(8,128)(2,1)} %bitcast.179, bf16[64,2,16,2,1024]{4,2,3,1,0:T(8,128)(2,1)} %gather_fusion.1), kind=kOutput, calls=%fused_computation.10.clone.1 | convolution fusion | flops 201326592 | bytes 10878976 | tf_op jit(solution)/shard_map/while/body/eval_jaxpr/tpim,pajm->ptiaj/dot_general | solution.py:98
  567.0 2.6 copy.111
  569.6 12.1 %fusion.38 = f32[64,3,16,2,16]{4,2,3,1,0:T(8,128)} fusion(bf16[3,64,16,2,1024]{4,2,0,1,3:T(8,128)(2,1)} %bitcast.180, bf16[64,2,16,2,1024]{4,2,3,1,0:T(8,128)(2,1)} %gather_fusion.1), kind=kOutput, calls=%fused_computation.12.clone.1 | convolution fusion | flops 201326592 | bytes 10878976 | tf_op jit(solution)/shard_map/while/body/eval_jaxpr/tpim,pajm->ptiaj/dot_general | solution.py:103
  581.7 3.3 copy.112
  586.2 12.1 %fusion.39 = f32[64,3,16,2,16]{4,2,3,1,0:T(8,128)} fusion(bf16[3,64,16,2,1024]{4,2,0,1,3:T(8,128)(2,1)} %bitcast.181, bf16[64,2,16,2,1024]{4,2,3,1,0:T(8,128)(2,1)} %gather_fusion.1), kind=kOutput, calls=%fused_computation.11.clone.1 | convolution fusion | flops 201326592 | bytes 10878976 | tf_op jit(solution)/shard_map/while/body/eval_jaxpr/tpim,pajm->ptiaj/dot_general | solution.py:109
  598.3 3.3 copy.113
  601.6 12.1 %fusion.40 = f32[64,3,16,2,16]{4,2,3,1,0:T(8,128)} fusion(bf16[3,64,16,2,1024]{4,2,0,1,3:T(8,128)(2,1)} %bitcast.182, bf16[64,2,16,2,1024]{4,2,3,1,0:T(8,128)(2,1)} %gather_fusion.1), kind=kOutput, calls=%fused_computation.9.clone.1 | convolution fusion | flops 201326592 | bytes 10878976 | tf_op jit(solution)/shard_map/while/body/eval_jaxpr/tpim,pajm->ptiaj/dot_general | solution.py:114
  613.7 3.3 copy.114
  623.8 2.1 constant_dynamic-update-slice_fusion.2
  625.9 4.0 broadcast_multiply_fusion
  (100 shorter events, 40.5 us)
Async XLA Ops:
  6.5 2.1 copy-start
  8.6 16.6 %collective-permute-start.1 = (bf16[1,1,2,128,2,1024]{3,5,4,2,1,0:T(8,128)(2,1)S(1)}, bf16[1,1,2,128,2,1024]{3,5,4,2,1,0:T(8,128)(2,1)S(1)}, u32[]{:S(2)}, u32[]{:S(2)}) collective-permute-start(bf16[1,1,2,128,2,1024]{3,5,4,2,1,0:T(8,128)(2,1)S(1)} %get-tuple-element.138), channel_id=1, source_target_pairs={{16,0},{32,16},{48,32},{64,48},{80,64},{96,80},{112,96},{128,112},... | collective-permute-start | bytes 3145736 | tf_op jit(solution)/shard_map/ppermute | solution.py:19
  12.9 19.7 %collective-permute-start = (bf16[1,1,2,128,2,1024]{3,5,4,2,1,0:T(8,128)(2,1)S(1)}, bf16[1,1,2,128,2,1024]{3,5,4,2,1,0:T(8,128)(2,1)S(1)}, u32[]{:S(2)}, u32[]{:S(2)}) collective-permute-start(bf16[1,1,2,128,2,1024]{3,5,4,2,1,0:T(8,128)(2,1)S(1)} %get-tuple-element.138), channel_id=1, source_target_pairs={{0,16},{16,32},{32,48},{48,64},{64,80},{80,96},{96,112},{112,128},... | collective-permute-start | bytes 3145736 | tf_op jit(solution)/shard_map/ppermute | solution.py:18
  25.2 158.5 %copy-start.1 = (bf16[1,1,2,128,2,1024]{3,5,4,2,1,0:T(8,128)(2,1)}, bf16[1,1,2,128,2,1024]{3,5,4,2,1,0:T(8,128)(2,1)S(1)}, u32[]{:S(2)}) copy-start(bf16[1,1,2,128,2,1024]{3,5,4,2,1,0:T(8,128)(2,1)S(1)} %collective-permute-done.1) | copy-start | bytes 3145732
  32.7 1.0 copy-start.2
  35.7 159.4 %collective-permute-start.3 = (bf16[3,1,2,128,2,1024]{3,5,4,2,1,0:T(8,128)(2,1)}, bf16[3,1,2,128,2,1024]{3,5,4,2,1,0:T(8,128)(2,1)}, u32[]{:S(2)}, u32[]{:S(2)}) collective-permute-start(bf16[3,1,2,128,2,1024]{3,5,4,2,1,0:T(8,128)(2,1)} %pad_maximum_fusion.2), channel_id=1, source_target_pairs={{1,0},{2,1},{3,2},{4,3},{5,4},{6,5},{7,6},{8,7},{9,8},{10,9},{11,1... | collective-permute-start | bytes 9437192 | tf_op jit(solution)/shard_map/ppermute | solution.py:19
  37.0 158.1 %collective-permute-start.2 = (bf16[3,1,2,128,2,1024]{3,5,4,2,1,0:T(8,128)(2,1)}, bf16[3,1,2,128,2,1024]{3,5,4,2,1,0:T(8,128)(2,1)}, u32[]{:S(2)}, u32[]{:S(2)}) collective-permute-start(bf16[3,1,2,128,2,1024]{3,5,4,2,1,0:T(8,128)(2,1)} %pad_maximum_fusion.2), channel_id=1, source_target_pairs={{0,1},{1,2},{2,3},{3,4},{4,5},{5,6},{6,7},{7,8},{8,9},{9,10},{10,1... | collective-permute-start | bytes 9437192 | tf_op jit(solution)/shard_map/ppermute | solution.py:18
  177.3 6.4 %copy-start.3 = (s32[1,1,3,256]{3,1,2,0:T(1,128)S(1)}, s32[1,1,3,256]{3,1,2,0:T(1,128)}, u32[]{:S(2)}) copy-start(s32[1,1,3,256]{3,1,2,0:T(1,128)} %param.10) | copy-start | bytes 9220
  231.8 394.0 %copy-start.4 = (f32[256]{0:T(256)S(1)}, f32[256]{0:T(256)}, u32[]{:S(2)}) copy-start(f32[256]{0:T(256)} %compare_convert_fusion) | copy-start | bytes 3076
where the time goes:
time: 634 us; the launch traced here: 630 us
  local copies, waits for them, and re-layouts  224 us (35%)
  matrix products  198 us (31%)
  blocking collectives  133 us (21%)
  other arithmetic  38.7 us (6%)
  waiting for transfers between devices  17.8 us (3%)
  starting transfers between devices  13.7 us (2%)
    psum x1, blocking collectives, per_device(): lax.psum((power, station_count[0, 0].astype(jnp.float32)), ('lat', 'lon'))  133 us
    gather x8, local copies, waits for them, and re-layouts, one_group(): targets = target_view[:, local_blocks]  72.1 us
    dot_general x4, matrix products, one_group(): jnp.einsum('tpim,pajm->ptiaj', targets[:, :, :, 1], partners[:, :, :, 0],...  48.4 us
    dot_general x4, matrix products, one_group(): jnp.einsum('tpim,pajm->ptiaj', targets[:, :, :, 1], partners[:, :, :, 1],...  48.4 us
    dot_general x4, matrix products, one_group(): jnp.einsum('tpim,pajm->ptiaj', targets[:, :, :, 0], partners[:, :, :, 0],...  48.3 us
    dot_general x4, matrix products, one_group(): jnp.einsum('tpim,pajm->ptiaj', targets[:, :, :, 0], partners[:, :, :, 1],...  48.3 us
    gather x4, local copies, waits for them, and re-layouts, one_group(): partners = near_view[offsets, :, near_index]  37.9 us
    dynamic_update_slice x8, local copies, waits for them, and re-layouts, per_device(): solved = lax.map(one_group, batches).reshape(pairs, 12, block * block)  13.6 us
  transfers between devices with their start and end apart: 4, of which 2 were waited for; matrix products, arithmetic and copies ran while one was open for 3% of the time, Pallas kernels for 0%

commit v1 on v0

v1 whole, which is shorter than its diff:
```python
import functools
import math

import jax
import jax.numpy as jnp
import ml_dtypes
import numpy as np
from jax import lax
from jax.experimental import pallas as pl
from jax.experimental.pallas import tpu as pltpu
from jax.sharding import PartitionSpec as P

BLOCK = 16
SLOTS = 128
WIN = 64
LEN = 128
NBAND = 16
GROUPS = 8
BLOCKS = SLOTS // BLOCK
F32 = jnp.float32
BF16 = jnp.bfloat16


def dft_matrix():
    samples = np.arange(LEN)
    bins = np.arange(LEN // 2)
    phase = (samples[:, None] * bins[None]) % LEN
    angle = phase.astype(np.float32) * np.float32(2.0 * math.pi / LEN)
    factor = np.float32(1.0 / math.sqrt(LEN))
    both = np.concatenate([np.cos(angle) * factor, -np.sin(angle) * factor], axis=1)
    return both.astype(ml_dtypes.bfloat16)


def nt_dot(a, b):
    return lax.dot_general(a, b, (((1,), (1,)), ((), ())), preferred_element_type=F32)


def group_transpose(parts):
    lane = lax.broadcasted_iota(jnp.int32, parts[0].shape, 1)
    group = lane // BLOCK
    v = [x if i == 0 else pltpu.roll(x, i * BLOCK, 1) for i, x in enumerate(parts)]
    for bit in (1, 2, 4):
        mask = (group // bit) % 2 == 1
        v = [jnp.where(mask, v[(k + bit) % 8], v[k]) for k in range(8)]
    out = []
    for q in range(8):
        x = v[(-q) % 8]
        out.append(x if q == 0 else pltpu.roll(x, LEN - q * BLOCK, 1))
    return out


def kernel(
    n_lat, n_lon, dims,
    count_ref, pairs_ref, list_ref, bins_ref, dft_ref, series_ref, out_ref,
    xbuf, tab, own, near, lhs, gram, red_send, red_recv, cross, solved,
    series_sem, own_send, fwd_send, lon_recv, lat_recv,
    gown_send, gfwd_send, gram_recv, rsend, rrecv,
):
    lat, lon = lax.axis_index("lat"), lax.axis_index("lon")
    has_up, has_down = lat > 0, lat < n_lat - 1
    has_left, has_right = lon > 0, lon < n_lon - 1

    def dev(la, lo):
        return (la, lo)

    steps = []
    bit = 1
    while bit < n_lat:
        steps.append(("lat", bit))
        bit *= 2
    bit = 1
    while bit < n_lon:
        steps.append(("lon", bit))
        bit *= 2

    def partner(step):
        axis, b = step
        if axis == "lat":
            return dev(lat + b * (1 - 2 * ((lat // b) % 2)), lon)
        return dev(lat, lon + b * (1 - 2 * ((lon // b) % 2)))

    sides = (
        (has_up, dev(lat - 1, lon)),
        (has_down, dev(lat + 1, lon)),
        (has_left, dev(lat, lon - 1)),
        (has_right, dev(lat, lon + 1)),
    )
    MESH = pl.DeviceIdType.MESH
    barrier = pltpu.get_barrier_semaphore()
    for here, target in sides:
        @pl.when(here)
        def _(target=target):
            pl.semaphore_signal(barrier, inc=1, device_id=target, device_id_type=MESH)
    for step in steps:
        pl.semaphore_signal(barrier, inc=1, device_id=partner(step), device_id_type=MESH)

    def series_copy(g):
        return pltpu.make_async_copy(
            series_ref.at[:, pl.ds(g * 8, 8)], xbuf.at[:, pl.ds(g * 8, 8)], series_sem.at[g]
        )

    for g in range(GROUPS):
        series_copy(g).start()

    lane = lax.broadcasted_iota(jnp.int32, (LEN, 256), 1)
    row = lax.broadcasted_iota(jnp.int32, (LEN, 256), 0)
    bins = jnp.zeros((LEN, 256), jnp.int32)
    for k in range(NBAND):
        bins = jnp.where(lane % NBAND == k, bins_ref[k], bins)
    chosen = (row % 64 == bins) & (row // 64 == lane // 128)
    full = jnp.dot(dft_ref[...], chosen.astype(F32).astype(BF16), preferred_element_type=F32)
    window = (lane // NBAND) % 8
    for j in range(4):
        for h in range(2):
            tab[j, h * LEN:(h + 1) * LEN, :] = jnp.where(window == 2 * j + h, full, 0.0).astype(BF16)
    prow = lax.broadcasted_iota(jnp.int32, (SLOTS, SLOTS), 0)
    pcol = lax.broadcasted_iota(jnp.int32, (SLOTS, SLOTS), 1)
    diagonal = pcol == (prow % BLOCKS) * BLOCK + prow // BLOCKS
    permute = diagonal.astype(F32).astype(BF16)
    live = row < count_ref[0, 0]

    def clear(o):
        near[o] = jnp.zeros(near.shape[1:], BF16)
        gram[o] = jnp.zeros(gram.shape[1:], F32)

    for o in range(9):
        di, dj = o // 3 - 1, o % 3 - 1
        if o == 4:
            continue
        inside = (lat + di >= 0) & (lat + di < n_lat) & (lon + dj >= 0) & (lon + dj < n_lon)

        @pl.when(jnp.logical_not(inside))
        def _(o=o):
            clear(o)

    here_count = (
        has_up.astype(jnp.int32) + has_down.astype(jnp.int32)
        + has_left.astype(jnp.int32) + has_right.astype(jnp.int32)
    )
    pl.semaphore_wait(barrier, here_count + len(steps))

    slots = (7, 1, 5, 3)

    def own_copy(side, g):
        piece = own if g is None else own.at[g]
        slot = near.at[slots[side]] if g is None else near.at[slots[side], g]
        sem = lon_recv.at[side - 2, 0 if g is None else g] if side >= 2 else lat_recv.at[slots[side]]
        return pltpu.make_async_remote_copy(
            src_ref=piece, dst_ref=slot, send_sem=own_send.at[side], recv_sem=sem,
            device_id=sides[side][1], device_id_type=MESH,
        )

    def spectra_step(g, _):
        series_copy(g).wait()
        for c in range(3):
            total = None
            for j in range(4):
                x = jnp.concatenate([xbuf[c, g * 8 + 2 * j], xbuf[c, g * 8 + 2 * j + 1]], axis=1)
                part = jnp.dot(x, tab[j], preferred_element_type=F32)
                total = part if total is None else total + part
            spec = jnp.where(live, total, 0.0).astype(BF16)
            if c < 2:
                own[g, c * SLOTS:(c + 1) * SLOTS, :] = spec
            mixed = jnp.dot(permute, spec, preferred_element_type=F32).astype(BF16)
            lhs[g, c * SLOTS:(c + 1) * SLOTS, :] = mixed
            lhs[g, 384 + c * SLOTS:384 + (c + 1) * SLOTS, 0:128] = mixed[:, 128:256]
            lhs[g, 384 + c * SLOTS:384 + (c + 1) * SLOTS, 128:256] = -mixed[:, 0:128]
        for side in range(4):
            @pl.when(sides[side][0])
            def _(side=side):
                own_copy(side, g).start()
        return 0

    lax.fori_loop(0, GROUPS, spectra_step, 0)

    def cross_block(source):
        for m in range(3):
            total = None
            for g in range(GROUPS):
                part = nt_dot(lhs[g, m * 256:(m + 1) * 256, :], source(g))
                total = part if total is None else total + part
            cross[m * 256:(m + 1) * 256, :] = total

    def pick(r, t, a):
        block = cross[r * 384 + t * 128:r * 384 + (t + 1) * 128, a * 128:(a + 1) * 128]
        return jnp.sum(jnp.where(diagonal, block, 0.0), axis=0, keepdims=True)

    cross_block(lambda g: own[g])
    gxx, gyy, gre, gim = pick(0, 0, 0), pick(0, 1, 1), pick(0, 1, 0), pick(1, 1, 0)
    gram[4] = jnp.concatenate([gxx, gyy, gre, gim, gxx, gyy, gre, gim], axis=0)
    power = 0.5 * jnp.sum(gxx + gyy, axis=1, keepdims=True)
    srow = lax.broadcasted_iota(jnp.int32, (8, 128), 0)
    count = count_ref[0, 0].astype(F32)
    red_send[0] = jnp.where(srow == 0, jnp.broadcast_to(power, (8, 128)), count)

    def gram_copy(side):
        return pltpu.make_async_remote_copy(
            src_ref=gram.at[4], dst_ref=gram.at[slots[side]], send_sem=gown_send.at[side],
            recv_sem=gram_recv.at[slots[side]], device_id=sides[side][1], device_id_type=MESH,
        )

    for side in range(4):
        @pl.when(sides[side][0])
        def _(side=side):
            gram_copy(side).start()

    forwards = ((3, 0, 6), (3, 1, 0), (5, 0, 8), (5, 1, 2))

    def fwd_copy(f, g):
        source, side, slot = forwards[f]
        return pltpu.make_async_remote_copy(
            src_ref=near.at[source] if g is None else near.at[source, g],
            dst_ref=near.at[slot] if g is None else near.at[slot, g],
            send_sem=fwd_send.at[f], recv_sem=lat_recv.at[slot],
            device_id=sides[side][1], device_id_type=MESH,
        )

    def fwd_gram(f):
        source, side, slot = forwards[f]
        return pltpu.make_async_remote_copy(
            src_ref=gram.at[source], dst_ref=gram.at[slot], send_sem=gfwd_send.at[f],
            recv_sem=gram_recv.at[slot], device_id=sides[side][1], device_id_type=MESH,
        )

    def each_forward(action):
        for f, (source, side, _) in enumerate(forwards):
            has_source = has_left if source == 3 else has_right

            @pl.when(has_source & sides[side][0])
            def _(f=f):
                action(f)

    arrivals = ((3, has_left, 1), (5, has_right, 0))

    def lon_wait(slot, index, g):
        pltpu.make_async_remote_copy(
            src_ref=near.at[slot, g], dst_ref=near.at[slot, g], send_sem=own_send.at[0],
            recv_sem=lon_recv.at[index, g], device_id=sides[0][1], device_id_type=MESH,
        ).wait_recv()

    def gram_wait(slot):
        pltpu.make_async_remote_copy(
            src_ref=gram.at[slot], dst_ref=gram.at[slot], send_sem=gown_send.at[0],
            recv_sem=gram_recv.at[slot], device_id=sides[0][1], device_id_type=MESH,
        ).wait_recv()

    def reduce_start(s):
        pltpu.make_async_remote_copy(
            src_ref=red_send.at[s], dst_ref=red_recv.at[s], send_sem=rsend.at[s], recv_sem=rrecv.at[s],
            device_id=partner(steps[s]), device_id_type=MESH,
        ).start()

    def reduce_end(s):
        pltpu.make_async_remote_copy(
            src_ref=red_send.at[s], dst_ref=red_recv.at[s], send_sem=rsend.at[s], recv_sem=rrecv.at[s],
            device_id=partner(steps[s]), device_id_type=MESH,
        ).wait()
        red_send[s + 1] = red_send[s] + red_recv[s]

    for slot, here, _ in arrivals:
        @pl.when(here)
        def _(slot=slot):
            gram_wait(slot)
    each_forward(lambda f: fwd_gram(f).start())

    for g in range(GROUPS):
        if g < len(steps):
            reduce_start(g)
        for slot, here, index in arrivals:
            @pl.when(here)
            def _(slot=slot, index=index, g=g):
                lon_wait(slot, index, g)
            for f, (source, side, _) in enumerate(forwards):
                if source == slot:
                    @pl.when(here & sides[side][0])
                    def _(f=f, g=g):
                        fwd_copy(f, g).start()
        if g < len(steps):
            reduce_end(g)

    total = red_send[len(steps)]
    ridge = total[0:1, :] / total[1:2, :] + 1e-06

    def solve_tile(o):
        terms = gram[o]
        upper = terms[0:1] + ridge
        lower = terms[1:2] + ridge
        gre, gim = terms[2:3], terms[3:4]
        inverse = 1.0 / (upper * lower - (gre * gre + gim * gim))
        wide = lambda v: jnp.broadcast_to(v * inverse, (8, 128))
        upper, lower, gre, gim = wide(upper), wide(lower), wide(gre), wide(gim)
        for t in range(3):
            for half in range(2):
                parts = [[], [], [], []]
                for i in range(8):
                    base = t * 128 + (half * 8 + i) * 8
                    first_re = cross[base:base + 8, 0:128]
                    second_re = cross[base:base + 8, 128:256]
                    first_im = cross[384 + base:384 + base + 8, 0:128]
                    second_im = cross[384 + base:384 + base + 8, 128:256]
                    parts[0].append(lower * first_re - (gre * second_re - gim * second_im))
                    parts[1].append(lower * first_im - (gre * second_im + gim * second_re))
                    parts[2].append(upper * second_re - (gre * first_re + gim * first_im))
                    parts[3].append(upper * second_im - (gre * first_im - gim * first_re))
                for ar in range(4):
                    plane = ((ar // 2) * 3 + t) * 2 + ar % 2
                    moved = group_transpose(parts[ar])
                    for q in range(8):
                        solved[plane, pl.ds(o * 64 + q * 8, 8), half * 128:(half + 1) * 128] = moved[q]

    solve_own = lambda: solve_tile(4)
    solve_own()

    even = lat % 2 == 0
    fast = jnp.where(even, 2, 0)
    slow = 2 - fast

    def tile_step(k, _):
        is_slow = (k == 3) | (k >= 6)
        di = jnp.where(k < 2, 1, jnp.where(is_slow, slow, fast))
        dj = jnp.where(k < 2, 2 * k, jnp.where(k < 4, 1, 2 * (k % 2)))
        o = di * 3 + dj
        la, lo = lat + di - 1, lon + dj - 1
        inside = (la >= 0) & (la < n_lat) & (lo >= 0) & (lo < n_lon)

        @pl.when(inside & (k >= 2))
        def _():
            pltpu.make_async_remote_copy(
                src_ref=near.at[o], dst_ref=near.at[o], send_sem=own_send.at[0],
                recv_sem=lat_recv.at[o], device_id=sides[0][1], device_id_type=MESH,
            ).wait_recv()
            gram_wait(o)
        cross_block(lambda g: near[o, g])
        solve_tile(o)
        return 0

    lax.fori_loop(0, 8, tile_step, 0)

    for plane in range(12):
        solved[plane, 576:584, :] = jnp.zeros((8, 256), F32)
    live_pairs = pairs_ref[0, 0]

    def gather_step(e, _):
        source = list_ref[0, e] * 64 + list_ref[2, e] * 8 + list_ref[1, e]
        source = jnp.where(e < live_pairs, source, 576)
        for plane in range(12):
            out_ref[plane, pl.ds(e, 1), :] = solved[plane, pl.ds(source, 1), :]
        return 0

    lax.fori_loop(0, dims[0], gather_step, 0)

    for side in range(4):
        @pl.when(sides[side][0])
        def _(side=side):
            own_copy(side, None).wait_send()
            gram_copy(side).wait_send()

    def finish(f):
        fwd_copy(f, None).wait_send()
        fwd_gram(f).wait_send()

    each_forward(finish)


def per_device(n_lat, n_lon, series, station_count, pair_count, pair_list, band_bins):
    pairs = pair_list.shape[-1]
    smem = pl.BlockSpec(memory_space=pltpu.SMEM)
    vmem = pl.BlockSpec(memory_space=pltpu.VMEM)
    steps = (n_lat - 1).bit_length() + (n_lon - 1).bit_length()
    dma = pltpu.SemaphoreType.DMA
    solved = pl.pallas_call(
        functools.partial(kernel, n_lat, n_lon, (pairs,)),
        out_shape=jax.ShapeDtypeStruct((12, pairs, BLOCK * BLOCK), F32),
        in_specs=[smem, smem, smem, smem, vmem, pl.BlockSpec(memory_space=pl.ANY)],
        out_specs=vmem,
        scratch_shapes=[
            pltpu.VMEM((3, WIN, SLOTS, LEN), BF16),
            pltpu.VMEM((4, 2 * LEN, 256), BF16),
            pltpu.VMEM((GROUPS, 256, 256), BF16),
            pltpu.VMEM((9, GROUPS, 256, 256), BF16),
            pltpu.VMEM((GROUPS, 768, 256), BF16),
            pltpu.VMEM((9, 8, 128), F32),
            pltpu.VMEM((steps + 1, 8, 128), F32),
            pltpu.VMEM((steps, 8, 128), F32),
            pltpu.VMEM((768, 256), F32),
            pltpu.VMEM((12, 584, 256), F32),
            dma((GROUPS,)),
            dma((4,)),
            dma((4,)),
            dma((2, GROUPS)),
            dma((9,)),
            dma((4,)),
            dma((4,)),
            dma((9,)),
            dma((steps,)),
            dma((steps,)),
        ],
        compiler_params=pltpu.CompilerParams(
            collective_id=0, has_side_effects=True, vmem_limit_bytes=56 * 1024 * 1024
        ),
    )(
        station_count,
        pair_count,
        pair_list.reshape(3, pairs),
        band_bins,
        jnp.asarray(dft_matrix()),
        series.reshape(3, WIN, SLOTS, LEN),
    )
    return solved.transpose(1, 0, 2)[None, None]


def solution(mesh):
    in_specs = (
        P("lat", "lon", None, None, None, None),
        P("lat", "lon"),
        P("lat", "lon"),
        P("lat", "lon", None, None),
        P(),
    )
    out_specs = P("lat", "lon", None, None, None)
    return jax.shard_map(
        functools.partial(per_device, mesh.shape["lat"], mesh.shape["lon"]),
        mesh=mesh, in_specs=in_specs, out_specs=out_specs, check_vma=False,
    )
```

time: 634 us -> 88.9 us (0.14)
  local copies, waits for them, and re-layouts: 224 us -> 5.03 us
  matrix products: 198 us -> 0 us
  blocking collectives: 133 us -> 0 us
  Pallas kernels: 0 us -> 81.2 us
  other arithmetic: 38.7 us -> 0 us
  waiting for transfers between devices: 17.8 us -> 0 us
  starting transfers between devices: 13.7 us -> 0 us
    dot_general x17 -> x0, matrix products: 198 us -> none  [the longest x4 48.4 us: one_group(): jnp.einsum('tpim,pajm->ptiaj', targets[:, :, :, 1], partners[:, :, :, 0],...]
    psum x1 -> x0, blocking collectives: 133 us -> none  [per_device(): lax.psum((power, station_count[0, 0].astype(jnp.float32)), ('lat', 'lon'))]
    gather x36 -> x0, local copies, waits for them, and re-layouts: 123 us -> none  [the longest x8 72.1 us: one_group(): targets = target_view[:, local_blocks]]
    pallas_call x0 -> x1, Pallas kernels: none -> 81.2 us  [per_device(): pl.pallas_call(functools.partial(kernel, n_lat, n_lon, (pairs,)), out_sha...]
    dot_general x16 -> x0, local copies, waits for them, and re-layouts: 49.7 us -> none  [the longest x4 13.2 us: one_group(): jnp.einsum('tpim,pajm->ptiaj', targets[:, :, :, 1], partners[:, :, :, 1],...]
    ppermute x4 -> x0, waiting for transfers between devices: 17.8 us -> none  [the longest x2 10.4 us: with_halo(): after = lax.ppermute(initial, axis, down)]
    ppermute x4 -> x0, starting transfers between devices: 13.7 us -> none  [the longest x2 8.15 us: with_halo(): before = lax.ppermute(last, axis, up)]
    dynamic_update_slice x8 -> x0, local copies, waits for them, and re-layouts: 13.6 us -> none  [per_device(): solved = lax.map(one_group, batches).reshape(pairs, 12, block * block)]
  transfers between devices with their start and end apart: 4 -> 0, of which waited for: 2 -> 0; matrix products, arithmetic and copies ran while one was open for 3% -> 0% of each run, Pallas kernels for 0% -> 0%
where the time goes in v1:
time: 88.9 us; the launch traced here: 87.6 us
  Pallas kernels  81.2 us (91%)
  local copies, waits for them, and re-layouts  5.03 us (6%)
  between operations  1.31 us (1%)
    pallas_call x1, Pallas kernels, per_device(): pl.pallas_call(functools.partial(kernel, n_lat, n_lon, (pairs,)), out_sha...  81.2 us
    unnamed x2, local copies, waits for them, and re-layouts  5.03 us

profile of v1, /device:TPU:4, one launch (start us, length us, event | category | flops | bytes accessed | tf_op | source)
XLA Modules:
  0.0 87.6 jit_solution(4887236665471444669)
XLA Ops:
  1.3 1.3 %copy.9 = s32[1,1,3,256]{3,2,1,0:T(4,128)} copy(s32[1,1,3,256]{3,1,2,0:T(1,128)} %param.9) | data formatting | bytes 6144
  2.6 81.2 %shard_map.64 = f32[12,256,256]{2,1,0:T(8,128)} custom-call(s32[1,1]{1,0:T(1,128)S(6)} %copy.11.count_ref, s32[1,1]{1,0:T(1,128)S(6)} %copy.12.pairs_ref, s32[3,256]{1,0:T(4,128)} %bitcast.9, s32[16]{0:T(128)} %bins_ref.1, bf16[128,128]{1,0:T(8,128)(2,1)} %constant.2.clone.dft_ref, bf16[3,64,128,128]{3,2,1,0:T(8,128)(2,1)} %bitcast.8), custom_call_target="tpu_custom_call" | custom-call | tf_op jit(solution)/shard_map/pallas_call | solution.py:371
  83.8 3.8 %copy.13 = f32[1,1,256,12,256]{4,2,3,1,0:T(8,128)} copy(f32[1,1,256,12,256]{4,2,3,1,0:T(8,128)} %bitcast.7) | data formatting | bytes 6291456

commit v2 on v0

v2 whole, which is shorter than its diff:
```python
import functools
import math

import jax
import jax.numpy as jnp
import ml_dtypes
import numpy as np
from jax import lax
from jax.experimental import pallas as pl
from jax.experimental.pallas import tpu as pltpu
from jax.sharding import PartitionSpec as P

BLOCK = 16
SLOTS = 128
WIN = 64
LEN = 128
NBAND = 16
GROUPS = 8
FIRST = 1
AHEAD = 2
EARLY = 0
F32 = jnp.float32
BF16 = jnp.bfloat16
MESH = pl.DeviceIdType.MESH

LEFT, RIGHT, FAST, SLOW, FAST_LEFT, FAST_RIGHT, SLOW_LEFT, SLOW_RIGHT, OWN = range(9)


def dft_matrix():
    samples = np.arange(LEN)
    bins = np.arange(LEN // 2)
    phase = (samples[:, None] * bins[None]) % LEN
    angle = phase.astype(np.float32) * np.float32(2.0 * math.pi / LEN)
    factor = np.float32(1.0 / math.sqrt(LEN))
    both = np.concatenate([np.cos(angle) * factor, -np.sin(angle) * factor], axis=1)
    return both.astype(ml_dtypes.bfloat16)


def nt_dot(a, b):
    return lax.dot_general(a, b, (((1,), (1,)), ((), ())), preferred_element_type=F32)


def group_transpose(parts, masks):
    def skew(v):
        for bit, mask in zip((1, 2, 4), masks):
            v = [jnp.where(mask, v[(k + bit) % 8], v[k]) for k in range(8)]
        return v

    v = [x if d == 0 else pltpu.roll(x, d * BLOCK, 1) for d, x in enumerate(skew(parts))]
    v = skew(v)
    return [v[(-q) % 8] for q in range(8)]


def kernel(
    n_lat, n_lon, pairs,
    count_ref, pairs_ref, bins_ref, list_ref, dft_ref, series_ref, out_ref,
    xbuf, tab, near, lhs, gram, power_ref, red_send, red_recv, a_recv, z_recv, cross, picked, code_ref, coef_ref,
    series_sem, near_recv, own_send, fwd_send, gram_recv, gown_send, gfwd_send, rsend, rrecv, a_send_sem, a_recv_sem, z_send_sem, z_recv_sem,
):
    lat, lon = lax.axis_index("lat"), lax.axis_index("lon")
    parity = lat % 2
    fast_lat = lat + 1 - 2 * parity
    slow_lat = lat - 1 + 2 * parity
    has_slow = (slow_lat >= 0) & (slow_lat < n_lat)
    has_left, has_right = lon > 0, lon < n_lon - 1
    middle = (lat == n_lat // 2 - 1) | (lat == n_lat // 2)
    special = middle & ((lon == 0) | (lon == n_lon - 1))
    left_special = middle & (lon == 1)
    right_special = middle & (lon == n_lon - 2)

    left_dev, right_dev = (lat, lon - 1), (lat, lon + 1)
    fast_dev, slow_dev = (fast_lat, lon), (slow_lat, lon)
    sides = {LEFT: (has_left, left_dev), RIGHT: (has_right, right_dev),
             FAST: (None, fast_dev), SLOW: (has_slow, slow_dev)}
    lands = {LEFT: RIGHT, RIGHT: LEFT, FAST: FAST, SLOW: SLOW}

    def when(cond, action):
        if cond is None:
            action()
        else:
            pl.when(cond)(action)

    def both(*conds):
        conds = [c for c in conds if c is not None]
        total = None
        for c in conds:
            total = c if total is None else total & c
        return total

    half_lat, half_lon = n_lat // 2, n_lon // 2
    ys, zs = half_lat // 2, half_lon
    x_hi, y = lat // half_lat, lat % half_lat // 2
    x_lo, z = lon // half_lon, lon % half_lon

    def across(d):
        x = (2 * x_hi + x_lo + d % 4) % 4
        return (x // 2 * half_lat + y * 2 + (parity + d // 4) % 2, x % 2 * half_lon + z)

    def along_z(d):
        return (lat, x_lo * half_lon + (z + d) % zs)

    def along_y(d):
        return (x_hi * half_lat + (y + d + ys) % ys * 2 + parity, lon)

    stages = [((1, -1) if k < (ys - 1) // 2 else (1,), k > 0) for k in range(ys // 2)]
    rings = [along_y(d) for d in ((1, -1) if ys > 1 else ())]
    rings += [across(d) for d in range(1, 8)] + [along_z(d) for d in range(1, zs)]

    barrier = pltpu.get_barrier_semaphore()

    def greet(target):
        pl.semaphore_signal(barrier, inc=1, device_id=target, device_id_type=MESH)

    gram[...] = jnp.zeros((9, 8, 128), F32)
    for here, target in sides.values():
        when(here, functools.partial(greet, target))
    for target in rings:
        greet(target)

    def series_copy(g):
        return pltpu.make_async_copy(
            series_ref.at[:, pl.ds(g * 8, 8)], xbuf.at[:, pl.ds(g * 8, 8)], series_sem.at[g]
        )

    for g in range(GROUPS):
        series_copy(g).start()

    lane = lax.broadcasted_iota(jnp.int32, (LEN, 256), 1)
    row = lax.broadcasted_iota(jnp.int32, (LEN, 256), 0)
    bins = jnp.zeros((LEN, 256), jnp.int32)
    for k in range(NBAND):
        bins = jnp.where(lane % NBAND == k, bins_ref[k], bins)
    chosen = (row % 64 == bins) & (row // 64 == lane // 128)
    full = jnp.dot(dft_ref[...], chosen.astype(F32).astype(BF16), preferred_element_type=F32)
    window = (lane // NBAND) % 8
    for j in range(4):
        for h in range(2):
            tab[j, h * LEN:(h + 1) * LEN, :] = jnp.where(window == 2 * j + h, full, 0.0).astype(BF16)
    live = row < count_ref[0, 0]
    power_ref[...] = jnp.zeros((8, 256), F32)

    listing = list_ref[...].astype(F32)
    code = listing[0] * 64.0 + listing[2] * 8.0 + listing[1]
    entry = lax.broadcasted_iota(jnp.int32, (1, pairs), 1)
    code = jnp.where(entry < pairs_ref[0, 0], code, -1.0)
    code_ref[...] = jnp.broadcast_to(code, (128, pairs)).T

    greeted = (
        has_slow.astype(jnp.int32) + has_left.astype(jnp.int32) + has_right.astype(jnp.int32)
        + (1 + len(rings))
    )
    pl.semaphore_wait(barrier, greeted)

    def remote(src, dst, send, recv, device):
        return pltpu.make_async_remote_copy(
            src_ref=src, dst_ref=dst, send_sem=send, recv_sem=recv,
            device_id=device, device_id_type=MESH,
        )

    def own_copy(side, g):
        return remote(
            lhs.at[g, pl.ds(0, 256)], near.at[lands[side], g], own_send.at[side],
            near_recv.at[lands[side], g], sides[side][1],
        )

    def spectra_step(g, _):
        series_copy(g).wait()
        total = None
        for j in range(4):
            w = g * 8 + 2 * j
            x = jnp.concatenate(
                [xbuf[:, w].reshape(3 * SLOTS, LEN), xbuf[:, w + 1].reshape(3 * SLOTS, LEN)], axis=1
            )
            part = jnp.dot(x, tab[j], preferred_element_type=F32)
            total = part if total is None else total + part
        masked = jnp.where(live[None], total.reshape(3, SLOTS, 256), 0.0)
        spec = masked.reshape(3 * SLOTS, 256).astype(BF16)
        lhs[g, 0:384, :] = spec
        when(has_slow & (jnp.logical_not(middle) | (g < AHEAD)), lambda: own_copy(SLOW, g).start())
        own_copy(FAST, g).start()
        for side in (LEFT, RIGHT):
            when(sides[side][0] & (g < FIRST), lambda side=side: own_copy(side, g).start())
        lhs[g, 384:768, 0:128] = spec[:, 128:256]
        lhs[g, 384:768, 128:256] = -spec[:, 0:128]
        wide = spec[0:256].astype(F32)
        power_ref[...] += jnp.sum((wide * wide).reshape(32, 8, 256), axis=0)
        return 0

    lax.fori_loop(0, GROUPS, spectra_step, 0)

    srow = lax.broadcasted_iota(jnp.int32, (8, 128), 0)
    power = 0.5 * jnp.sum(power_ref[...], keepdims=True)
    count = count_ref[0, 0].astype(F32)
    red_send[0] = jnp.where(srow == 0, jnp.broadcast_to(power, (8, 128)), count)

    def across_copy(d):
        return remote(
            red_send.at[0], a_recv.at[d - 1], a_send_sem.at[d - 1], a_recv_sem.at[d - 1], across(d)
        )

    def z_copy(d):
        return remote(
            red_send.at[1], z_recv.at[d - 1], z_send_sem.at[d - 1], z_recv_sem.at[d - 1], along_z(d)
        )

    for d in range(1, 8):
        across_copy(d).start()

    def reduce_copy(s, n):
        directions, passed = stages[s]
        return remote(
            red_recv.at[s - 1, n] if passed else red_send.at[s + 2], red_recv.at[s, n],
            rsend.at[s, n], rrecv.at[s, n], along_y(directions[n]),
        )

    def reduce_start(s):
        for n in range(len(stages[s][0])):
            reduce_copy(s, n).start()

    def reduce_end(s):
        total = red_send[s + 2]
        for n in range(len(stages[s][0])):
            reduce_copy(s, n).wait()
            total = total + red_recv[s, n]
        red_send[s + 3] = total

    total = red_send[0]
    for d in range(1, 8):
        across_copy(d).wait()
        total = total + a_recv[d - 1]
    red_send[1] = total
    for d in range(1, zs):
        z_copy(d).start()

    @pl.when(middle)
    def _():
        for g in range(AHEAD, GROUPS):
            own_copy(SLOW, g).start()

    for m in range(3):
        total = None
        for g in range(GROUPS):
            part = nt_dot(lhs[g, m * 256:(m + 1) * 256, :], lhs[g, 0:256, :])
            total = part if total is None else total + part
        for a in range(2):
            cross[OWN, a, m * 256:(m + 1) * 256, :] = total[:, a * 128:(a + 1) * 128]
    diagonal = (
        lax.broadcasted_iota(jnp.int32, (SLOTS, SLOTS), 0)
        == lax.broadcasted_iota(jnp.int32, (SLOTS, SLOTS), 1)
    )

    def pick(r, t, a):
        block = cross[OWN, a, r * 384 + t * 128:r * 384 + (t + 1) * 128, :]
        return jnp.sum(jnp.where(diagonal, block, 0.0), axis=0, keepdims=True)

    gxx, gyy, gre, gim = pick(0, 0, 0), pick(0, 1, 1), pick(0, 1, 0), pick(1, 1, 0)
    gram[OWN] = jnp.concatenate([gxx, gyy, gre, gim, gxx, gyy, gre, gim], axis=0)

    def gram_copy(side):
        return remote(
            gram.at[OWN], gram.at[lands[side]], gown_send.at[side], gram_recv.at[lands[side]],
            sides[side][1],
        )

    for side in range(4):
        when(sides[side][0], lambda side=side: gram_copy(side).start())

    forwards = (
        (LEFT, FAST, FAST_LEFT), (RIGHT, FAST, FAST_RIGHT),
        (LEFT, SLOW, SLOW_LEFT), (RIGHT, SLOW, SLOW_RIGHT),
        (SLOW, LEFT, SLOW_RIGHT), (SLOW, RIGHT, SLOW_LEFT),
    )

    def fwd_copy(f, g, n=None):
        source, side, role = forwards[f]
        at = g if n is None else pl.ds(g, n)
        return remote(
            near.at[source, at], near.at[role, at], fwd_send.at[f],
            near_recv.at[role, g], sides[side][1],
        )

    def fwd_gram(f):
        source, side, role = forwards[f]
        return remote(
            gram.at[source], gram.at[role], gfwd_send.at[f], gram_recv.at[role], sides[side][1]
        )

    def arrived(role, g):
        remote(
            near.at[role, g], near.at[role, g], own_send.at[0], near_recv.at[role, g], fast_dev
        ).wait_recv()

    def gram_arrived(role):
        remote(
            gram.at[role], gram.at[role], gown_send.at[0], gram_recv.at[role], fast_dev
        ).wait_recv()

    def accumulate(role, g, n=1):
        for m in range(3):
            total = None
            for k in range(n):
                part = nt_dot(lhs[g + k, m * 256:(m + 1) * 256, :], near[role, g + k])
                total = part if total is None else total + part
            for a in range(2):
                cross[role, a, m * 256:(m + 1) * 256, :] += total[:, a * 128:(a + 1) * 128]

    total = red_send[1]
    for d in range(1, zs):
        z_copy(d).wait()
        total = total + z_recv[d - 1]
    red_send[2] = total
    for g in range(FIRST, AHEAD + FIRST):
        for side in (LEFT, RIGHT):
            when(sides[side][0], lambda side=side, g=g: own_copy(side, g).start())
    if stages:
        reduce_start(0)
    cross[0:8] = jnp.zeros((8, 2, 768, 128), F32)

    fast_base = (2 - 2 * parity) * 3
    slow_base = 2 * parity * 3
    tile_code = {
        OWN: 4, LEFT: 3, RIGHT: 5, FAST: fast_base + 1, SLOW: slow_base + 1,
        FAST_LEFT: fast_base, FAST_RIGHT: fast_base + 2,
        SLOW_LEFT: slow_base, SLOW_RIGHT: slow_base + 2,
    }

    lane = lax.broadcasted_iota(jnp.int32, (8, 128), 1)
    masks = [(lane & (BLOCK * bit)) != 0 for bit in (1, 2, 4)]

    def spread(role, h):
        for a in range(2):
            for t in range(3):
                for r in range(2):
                    for half in range(2):
                        column = ((a * 3 + t) * 2 + r) * 256 + half * 128
                        base = r * 384 + t * 128 + half * 8
                        moved = group_transpose(
                            [cross[role, a, pl.ds(base + i, 8, stride=BLOCK), :] for i in range(8)], masks
                        )
                        for q in range(0, 8, 2):
                            x = jnp.concatenate([moved[q], moved[q + 1]], axis=0)
                            high = x.astype(BF16)
                            low = (x - high.astype(F32)).astype(BF16)
                            at = pl.multiple_of(h * 128 + q * 8, 16)
                            picked[pl.ds(at, 16), column:column + 128] = high
                            at = pl.multiple_of(h * 128 + 64 + q * 8, 16)
                            picked[pl.ds(at, 16), column:column + 128] = low

    def gather(codes, first=None):
        index = lax.broadcasted_iota(jnp.int32, (pairs, 128), 1) % 64
        have = code_ref[...]
        hot = [
            jnp.where(have == (index + c * 64).astype(F32), 1.0, 0.0).astype(BF16) for c in codes
        ]
        hot = jnp.concatenate(hot, axis=1)
        for plane in range(12):
            out_ref[plane] += jnp.dot(
                hot, picked[:, plane * 256:(plane + 1) * 256], preferred_element_type=F32
            )

    def spread_two(first, second, codes):
        def tile(h, _):
            spread(jnp.where(h == 0, first, second), h)
            return 0
        lax.fori_loop(0, 2, tile, 0)
        gather(codes)

    def accumulate_roles(first, count, c, wait):
        def one(k, _):
            role = first + k + 2 * (k // 2)
            here = jnp.where(role % 2 == 0, has_left, has_right)
            if first == SLOW_LEFT:
                here = here & has_slow

            @pl.when(here)
            def _():
                @pl.when(role >= FAST_LEFT)
                def _():
                    arrived(role, c)
                    arrived(role, c + 1)
                accumulate(role, c, 2)
            return 0
        lax.fori_loop(0, count, one, 0)

    out_ref[...] = jnp.zeros(out_ref.shape, F32)

    def step(g, _):
        for s in range(len(stages) - 1):
            @pl.when(g == 7)
            def _(s=s):
                reduce_end(s)
                reduce_start(s + 1)

        @pl.when(has_slow & (g < 4) & jnp.logical_not(special))
        def _():
            for k in range(2):
                arrived(SLOW, 2 * g + k)

        for own_side, f_fast, f_slow, next_special, f_early in (
            (LEFT, 0, 2, left_special, 4), (RIGHT, 1, 3, right_special, 5),
        ):
            def service(own_side=own_side, f_fast=f_fast, f_slow=f_slow, next_special=next_special, f_early=f_early):
                when(g + AHEAD + FIRST < GROUPS, lambda: own_copy(own_side, g + AHEAD + FIRST).start())
                late = g + AHEAD + FIRST - GROUPS
                when(has_slow & (late >= 0) & (late < EARLY) & jnp.logical_not(special | next_special),
                     lambda: fwd_copy(f_early, late).start())
                arrived(own_side, g)
                when(has_slow & ((g >= EARLY) | next_special) & jnp.logical_not(special),
                     lambda: fwd_copy(f_slow, g).start())
                fwd_copy(f_fast, g).start()
            when(sides[own_side][0], service)

        @pl.when((left_special | right_special) & (g >= 4))
        def _():
            for k in range(2):
                c = 2 * (g - 4) + k
                when(left_special, lambda: fwd_copy(4, c).start())
                when(right_special, lambda: fwd_copy(5, c).start())

        @pl.when(g == GROUPS - 3)
        def _():
            for role, here in ((LEFT, has_left), (RIGHT, has_right)):
                when(here, lambda role=role: gram_arrived(role))
            for f in range(4):
                source, side, _ = forwards[f]
                when(both(sides[source][0], sides[side][0]), lambda f=f: fwd_gram(f).start())

        @pl.when(g % 2 == 1)
        def _():
            accumulate_roles(LEFT, 4, g - 1, True)

        @pl.when(g == 2)
        def _():
            for k in range(GROUPS):
                arrived(FAST, k)

        @pl.when((g == 2) | ((g == 4) & has_slow & jnp.logical_not(special)))
        def _():
            accumulate(jnp.where(g == 2, FAST, SLOW), 0, GROUPS)

        @pl.when((g == 5) | (g == 6))
        def _():
            spread_two(
                jnp.where(g == 5, OWN, slow_now), FAST,
                (jnp.where(g == 5, 4, slow_now_code), jnp.where(g == 5, tile_code[FAST], -5)),
            )

        @pl.when((g == 7) & has_slow & jnp.logical_not(special))
        def _():
            accumulate_roles(SLOW_LEFT, 2, 2, True)
        return 0

    lacks = jnp.where(has_left, SLOW_RIGHT, SLOW_LEFT)
    lacks_code = jnp.where(has_left, tile_code[SLOW_RIGHT], tile_code[SLOW_LEFT])
    slow_now = jnp.where(special, lacks, SLOW)
    slow_now_code = jnp.where(special, lacks_code, tile_code[SLOW])
    lax.fori_loop(0, GROUPS, step, 0)

    def pair_step(k, _):
        @pl.when((k == 1) & has_slow & jnp.logical_not(special))
        def _():
            accumulate_roles(SLOW_LEFT, 2, 4, True)

        @pl.when((k == 2) & has_slow)
        def _():
            def last_step(n, _):
                c = (2 * n + 2) % GROUPS
                accumulate_roles(SLOW_LEFT, 2, c, True)
                return 0
            lax.fori_loop(jnp.where(special, 0, 2), 4, last_step, 0)

            @pl.when(special)
            def _():
                for g in range(GROUPS):
                    arrived(SLOW, g)
                accumulate(SLOW, 0, GROUPS)

        first = jnp.where(k == 0, LEFT, jnp.where(k == 1, FAST_LEFT, SLOW_LEFT))
        code_a = jnp.where(k == 0, 3, jnp.where(k == 1, fast_base, slow_base))
        swap_a = (k == 2) & special & has_right
        swap_b = (k == 2) & special & has_left
        spread_two(
            jnp.where(swap_a, SLOW, first), jnp.where(swap_b, SLOW, first + 1),
            (jnp.where(swap_a, tile_code[SLOW], code_a), jnp.where(swap_b, tile_code[SLOW], code_a + 2)),
        )
        return 0

    lax.fori_loop(0, 3, pair_step, 0)

    if stages:
        reduce_end(len(stages) - 1)
    for role, here in (
        (FAST, None), (SLOW, has_slow), (FAST_LEFT, has_left), (FAST_RIGHT, has_right),
        (SLOW_LEFT, has_slow & has_left), (SLOW_RIGHT, has_slow & has_right),
    ):
        when(here, lambda role=role: gram_arrived(role))

    summed = red_send[len(stages) + 2]
    ridge = summed[0:1, :] / summed[1:2, :] + 1e-06
    upper = gram[:, 0, :] + ridge
    lower = gram[:, 1, :] + ridge
    gre, gim = gram[:, 2, :], gram[:, 3, :]
    inverse = 1.0 / (upper * lower - (gre * gre + gim * gim))
    row8 = lax.broadcasted_iota(jnp.int32, (8, 128), 0)
    own_block = row8 == lane // BLOCK
    repeat = (
        lax.broadcasted_iota(jnp.int32, (128, 128), 0) % BLOCK
        == lax.broadcasted_iota(jnp.int32, (128, 128), 1) % BLOCK
    ).astype(F32).astype(BF16)

    def split(x):
        high = x.astype(BF16)
        return high, (x - high.astype(F32)).astype(BF16)

    have = code_ref[...]
    blocks = jnp.floor(have * 0.125)
    index = lax.broadcasted_iota(jnp.int32, (pairs, 128), 1)
    order = [tile_code[r] for r in range(9)]
    wanted = jnp.full((1, 128), -5, jnp.int32)
    flat = lax.broadcasted_iota(jnp.int32, (1, 128), 1)
    for r in range(9):
        wanted = jnp.where(flat // 8 == r, order[r] * 8 + flat % 8, wanted)
    hot = jnp.where(blocks == wanted.astype(F32), 1.0, 0.0).astype(BF16)
    for n, value in enumerate((lower, upper, gre, gim)):
        value = value * inverse
        rows = [
            jnp.where(own_block, jnp.broadcast_to(value[r:r + 1], (8, 128)), 0.0) for r in range(9)
        ]
        rows = jnp.concatenate(rows + [jnp.zeros((56, 128), F32)], axis=0)
        high, low = split(rows)
        rows = (
            jnp.dot(high, repeat, preferred_element_type=F32)
            + jnp.dot(low, repeat, preferred_element_type=F32)
        )
        high, low = split(rows)
        coef_ref[n] = (
            jnp.dot(hot, high, preferred_element_type=F32)
            + jnp.dot(hot, low, preferred_element_type=F32)
        )

    def solve_step(e, _):
        at = pl.ds(pl.multiple_of(e * 32, 32), 32)
        lower, upper, gre, gim = coef_ref[0, at, :], coef_ref[1, at, :], coef_ref[2, at, :], coef_ref[3, at, :]
        for t in range(3):
            for half in range(2):
                lanes = slice(half * 128, (half + 1) * 128)
                first_re, first_im = out_ref[2 * t, at, lanes], out_ref[2 * t + 1, at, lanes]
                second_re, second_im = out_ref[6 + 2 * t, at, lanes], out_ref[7 + 2 * t, at, lanes]
                out_ref[2 * t, at, lanes] = lower * first_re - (gre * second_re - gim * second_im)
                out_ref[2 * t + 1, at, lanes] = lower * first_im - (gre * second_im + gim * second_re)
                out_ref[6 + 2 * t, at, lanes] = upper * second_re - (gre * first_re + gim * first_im)
                out_ref[7 + 2 * t, at, lanes] = upper * second_im - (gre * first_im - gim * first_re)
        return 0

    lax.fori_loop(0, pairs // 32, solve_step, 0)

    for side in range(4):
        def done(side=side):
            remote(
                near.at[0], near.at[0], own_send.at[side], near_recv.at[0, 0], fast_dev
            ).wait_send()
            gram_copy(side).wait_send()
        when(sides[side][0], done)
    for f, next_special in enumerate((None, None, left_special, right_special)):
        source, side, _ = forwards[f]

        def done(f=f, side=side, next_special=next_special):
            if side == FAST:
                fwd_copy(f, 0, GROUPS).wait_send()
            else:
                when(jnp.logical_not(special | next_special),
                     lambda: fwd_copy(f, EARLY, GROUPS - EARLY).wait_send())
                when(next_special, lambda: fwd_copy(f, 0, GROUPS).wait_send())
            fwd_gram(f).wait_send()
        when(both(sides[source][0], sides[side][0]), done)
    for f, here, next_special in ((4, has_left, left_special), (5, has_right, right_special)):
        when(has_slow & here & jnp.logical_not(special | next_special),
             lambda f=f: fwd_copy(f, 0, EARLY).wait_send())
        when(next_special, lambda f=f: fwd_copy(f, 0, GROUPS).wait_send())


def per_device(n_lat, n_lon, series, station_count, pair_count, pair_list, band_bins):
    pairs = pair_list.shape[-1]
    smem = pl.BlockSpec(memory_space=pltpu.SMEM)
    vmem = pl.BlockSpec(memory_space=pltpu.VMEM)
    stages = n_lat // 8
    zs = n_lon // 2
    dma = pltpu.SemaphoreType.DMA
    solved = pl.pallas_call(
        functools.partial(kernel, n_lat, n_lon, pairs),
        out_shape=pltpu.VMEM((12, pairs, BLOCK * BLOCK), F32),
        in_specs=[smem, smem, smem, vmem, vmem, pl.BlockSpec(memory_space=pl.ANY)],
        out_specs=vmem,
        scratch_shapes=[
            pltpu.VMEM((3, WIN, SLOTS, LEN), BF16),
            pltpu.VMEM((4, 2 * LEN, 256), BF16),
            pltpu.VMEM((8, GROUPS, 256, 256), BF16),
            pltpu.VMEM((GROUPS, 768, 256), BF16),
            pltpu.VMEM((9, 8, 128), F32),
            pltpu.VMEM((8, 256), F32),
            pltpu.VMEM((stages + 3, 8, 128), F32),
            pltpu.VMEM((max(stages, 1), 2, 8, 128), F32),
            pltpu.VMEM((7, 8, 128), F32),
            pltpu.VMEM((zs - 1, 8, 128), F32),
            pltpu.VMEM((9, 2, 768, 128), F32),
            pltpu.VMEM((256, 12 * 256), BF16),
            pltpu.VMEM((pairs, 128), F32),
            pltpu.VMEM((4, pairs, 128), F32),
            dma((GROUPS,)),
            dma((8, GROUPS)),
            dma((4,)),
            dma((6,)),
            dma((8,)),
            dma((4,)),
            dma((4,)),
            dma((max(stages, 1), 2)),
            dma((max(stages, 1), 2)),
            dma((7,)),
            dma((7,)),
            dma((zs - 1,)),
            dma((zs - 1,)),
        ],
        compiler_params=pltpu.CompilerParams(
            collective_id=0, has_side_effects=True, vmem_limit_bytes=56 * 1024 * 1024
        ),
    )(
        station_count,
        pair_count,
        band_bins,
        pair_list.reshape(3, 1, pairs),
        jnp.asarray(dft_matrix()),
        series.reshape(3, WIN, SLOTS, LEN),
    )
    return solved.transpose(1, 0, 2)[None, None]


def solution(mesh):
    in_specs = (
        P("lat", "lon", None, None, None, None),
        P("lat", "lon"),
        P("lat", "lon"),
        P("lat", "lon", None, None),
        P(),
    )
    out_specs = P("lat", "lon", None, None, None)
    return jax.shard_map(
        functools.partial(per_device, mesh.shape["lat"], mesh.shape["lon"]),
        mesh=mesh, in_specs=in_specs, out_specs=out_specs, check_vma=False,
    )
```

time: 634 us -> 62.3 us (0.10)
  local copies, waits for them, and re-layouts: 224 us -> 1.67 us
  matrix products: 198 us -> 0 us
  blocking collectives: 133 us -> 0 us
  Pallas kernels: 0 us -> 59.2 us
  other arithmetic: 38.7 us -> 0 us
  waiting for transfers between devices: 17.8 us -> 0 us
  starting transfers between devices: 13.7 us -> 0 us
    dot_general x17 -> x0, matrix products: 198 us -> none  [the longest x4 48.4 us: one_group(): jnp.einsum('tpim,pajm->ptiaj', targets[:, :, :, 1], partners[:, :, :, 0],...]
    psum x1 -> x0, blocking collectives: 133 us -> none  [per_device(): lax.psum((power, station_count[0, 0].astype(jnp.float32)), ('lat', 'lon'))]
    gather x36 -> x0, local copies, waits for them, and re-layouts: 123 us -> none  [the longest x8 72.1 us: one_group(): targets = target_view[:, local_blocks]]
    pallas_call x0 -> x1, Pallas kernels: none -> 59.2 us  [per_device(): pl.pallas_call(functools.partial(kernel, n_lat, n_lon, pairs), out_shape=...]
    dot_general x16 -> x0, local copies, waits for them, and re-layouts: 49.7 us -> none  [the longest x4 13.2 us: one_group(): jnp.einsum('tpim,pajm->ptiaj', targets[:, :, :, 1], partners[:, :, :, 1],...]
    ppermute x4 -> x0, waiting for transfers between devices: 17.8 us -> none  [the longest x2 10.4 us: with_halo(): after = lax.ppermute(initial, axis, down)]
    ppermute x4 -> x0, starting transfers between devices: 13.7 us -> none  [the longest x2 8.15 us: with_halo(): before = lax.ppermute(last, axis, up)]
    dynamic_update_slice x8 -> x0, local copies, waits for them, and re-layouts: 13.6 us -> none  [per_device(): solved = lax.map(one_group, batches).reshape(pairs, 12, block * block)]
  transfers between devices with their start and end apart: 4 -> 0, of which waited for: 2 -> 0; matrix products, arithmetic and copies ran while one was open for 3% -> 0% of each run, Pallas kernels for 0% -> 0%
where the time goes in v2:
time: 62.3 us; the launch traced here: 62.2 us
  Pallas kernels  59.2 us (95%)
  local copies, waits for them, and re-layouts  1.67 us (3%)
  between operations  1.3 us (2%)
    pallas_call x1, Pallas kernels, per_device(): pl.pallas_call(functools.partial(kernel, n_lat, n_lon, pairs), out_shape=...  59.2 us
    unnamed x1, local copies, waits for them, and re-layouts  1.67 us

profile of v2, /device:TPU:4, one launch (start us, length us, event | category | flops | bytes accessed | tf_op | source)
XLA Modules:
  0.0 62.2 jit_solution(3028937734476539498)
XLA Ops:
  1.3 59.2 %shard_map.64 = f32[12,256,256]{2,1,0:T(8,128)S(1)} custom-call(s32[1,1]{1,0:T(1,128)S(6)} %copy.9.count_ref, s32[1,1]{1,0:T(1,128)S(6)} %copy.10.pairs_ref, s32[16]{0:T(128)} %bins_ref.1, s32[3,1,256]{2,1,0:T(1,128)} %bitcast.7, bf16[128,128]{1,0:T(8,128)(2,1)} %constant.2.clone.dft_ref, bf16[3,64,128,128]{3,2,1,0:T(8,128)(2,1)} %bitcast.6), custom_call_target="tpu_custom_call" | custom-call | tf_op jit(solution)/shard_map/pallas_call | solution.py:589
  60.5 1.7 %copy.8 = f32[1,1,256,12,256]{4,2,3,1,0:T(8,128)} copy(f32[1,1,256,12,256]{4,2,3,1,0:T(8,128)S(1)} %bitcast.5) | data formatting | bytes 6291456

commit v3 on v2

--- a/solution.py
+++ b/solution.py
@@ -18,7 +18,7 @@
 GROUPS = 8
 FIRST = 1
 AHEAD = 2
-EARLY = 0
+EARLY, EARLY_MIDDLE = 1, 2
 F32 = jnp.float32
 BF16 = jnp.bfloat16
 MESH = pl.DeviceIdType.MESH
@@ -54,8 +54,8 @@
 def kernel(
     n_lat, n_lon, pairs,
     count_ref, pairs_ref, bins_ref, list_ref, dft_ref, series_ref, out_ref,
-    xbuf, tab, near, lhs, gram, power_ref, red_send, red_recv, a_recv, z_recv, cross, picked, code_ref, coef_ref,
-    series_sem, near_recv, own_send, fwd_send, gram_recv, gown_send, gfwd_send, rsend, rrecv, a_send_sem, a_recv_sem, z_send_sem, z_recv_sem,
+    xbuf, tab, near, lhs, gram, power_ref, red_send, red_recv, total_ref, z_recv, cross, picked, code_ref, coef_ref,
+    series_sem, near_recv, own_send, fwd_send, gram_recv, gown_send, gfwd_send, rsend, rrecv, z_send_sem, z_recv_sem, total_recv,
 ):
     lat, lon = lax.axis_index("lat"), lax.axis_index("lon")
     parity = lat % 2
@@ -65,6 +65,9 @@
     has_left, has_right = lon > 0, lon < n_lon - 1
     middle = (lat == n_lat // 2 - 1) | (lat == n_lat // 2)
     special = middle & ((lon == 0) | (lon == n_lon - 1))
+    edge = (lon == 0) | (lon == n_lon - 1)
+    early_here = jnp.where(middle, EARLY_MIDDLE, EARLY)
+    to_edge = {LEFT: lon == 1, RIGHT: lon == n_lon - 2}
     left_special = middle & (lon == 1)
     right_special = middle & (lon == n_lon - 2)
 
@@ -92,19 +95,25 @@
     x_hi, y = lat // half_lat, lat % half_lat // 2
     x_lo, z = lon // half_lon, lon % half_lon
 
-    def across(d):
-        x = (2 * x_hi + x_lo + d % 4) % 4
-        return (x // 2 * half_lat + y * 2 + (parity + d // 4) % 2, x % 2 * half_lon + z)
-
     def along_z(d):
-        return (lat, x_lo * half_lon + (z + d) % zs)
+        return (lat - parity + (parity + d // zs) % 2, x_lo * half_lon + (z + d % zs) % zs)
+
+    def along_x(d):
+        x = (2 * x_hi + x_lo + d + 4) % 4
+        return (x // 2 * half_lat + lat % half_lat, x % 2 * half_lon + z)
 
     def along_y(d):
         return (x_hi * half_lat + (y + d + ys) % ys * 2 + parity, lon)
 
-    stages = [((1, -1) if k < (ys - 1) // 2 else (1,), k > 0) for k in range(ys // 2)]
-    rings = [along_y(d) for d in ((1, -1) if ys > 1 else ())]
-    rings += [across(d) for d in range(1, 8)] + [along_z(d) for d in range(1, zs)]
+    stages = [
+        (find, (1, -1) if k < (size - 1) // 2 else (1,), k > 0)
+        for find, size in ((along_x, 4), (along_y, ys)) for k in range(size // 2)
+    ]
+    outer = ((z == 0) | (z == zs - 1)) if zs > 2 else z < 0
+    inner = jnp.logical_not(outer)
+    to_low, to_high = (z == 1) & inner, (z == zs - 2) & inner
+    rings = [along_x(1), along_x(-1)] + [along_y(d) for d in ((1, -1) if ys > 1 else ())]
+    rings += [along_z(d) for d in range(1, 2 * zs)]
 
     barrier = pltpu.get_barrier_semaphore()
 
@@ -139,12 +148,6 @@
     live = row < count_ref[0, 0]
     power_ref[...] = jnp.zeros((8, 256), F32)
 
-    listing = list_ref[...].astype(F32)
-    code = listing[0] * 64.0 + listing[2] * 8.0 + listing[1]
-    entry = lax.broadcasted_iota(jnp.int32, (1, pairs), 1)
-    code = jnp.where(entry < pairs_ref[0, 0], code, -1.0)
-    code_ref[...] = jnp.broadcast_to(code, (128, pairs)).T
-
     greeted = (
         has_slow.astype(jnp.int32) + has_left.astype(jnp.int32) + has_right.astype(jnp.int32)
         + (1 + len(rings))
@@ -176,7 +179,7 @@
         masked = jnp.where(live[None], total.reshape(3, SLOTS, 256), 0.0)
         spec = masked.reshape(3 * SLOTS, 256).astype(BF16)
         lhs[g, 0:384, :] = spec
-        when(has_slow & (jnp.logical_not(middle) | (g < AHEAD)), lambda: own_copy(SLOW, g).start())
+        when(has_slow, lambda: own_copy(SLOW, g).start())
         own_copy(FAST, g).start()
         for side in (LEFT, RIGHT):
             when(sides[side][0] & (g < FIRST), lambda side=side: own_copy(side, g).start())
@@ -193,49 +196,42 @@
     count = count_ref[0, 0].astype(F32)
     red_send[0] = jnp.where(srow == 0, jnp.broadcast_to(power, (8, 128)), count)
 
-    def across_copy(d):
-        return remote(
-            red_send.at[0], a_recv.at[d - 1], a_send_sem.at[d - 1], a_recv_sem.at[d - 1], across(d)
-        )
-
     def z_copy(d):
         return remote(
-            red_send.at[1], z_recv.at[d - 1], z_send_sem.at[d - 1], z_recv_sem.at[d - 1], along_z(d)
-        )
-
-    for d in range(1, 8):
-        across_copy(d).start()
+            red_send.at[0], z_recv.at[d - 1], z_send_sem.at[d - 1], z_recv_sem.at[d - 1], along_z(d)
+        )
+
+    for d in range(1, 2 * zs):
+        z_copy(d).start()
 
     def reduce_copy(s, n):
-        directions, passed = stages[s]
+        find, directions, passed = stages[s]
         return remote(
-            red_recv.at[s - 1, n] if passed else red_send.at[s + 2], red_recv.at[s, n],
-            rsend.at[s, n], rrecv.at[s, n], along_y(directions[n]),
+            red_recv.at[s - 1, n] if passed else red_send.at[s + 1], red_recv.at[s, n],
+            rsend.at[s, n], rrecv.at[s, n], find(directions[n]),
+        )
+
+    def total_copy(d):
+        return remote(
+            red_send.at[len(stages) + 1], total_ref, z_send_sem.at[0], total_recv, along_z(d + zs if d < 0 else d)
         )
 
     def reduce_start(s):
-        for n in range(len(stages[s][0])):
+        for n in range(len(stages[s][1])):
             reduce_copy(s, n).start()
 
     def reduce_end(s):
-        total = red_send[s + 2]
-        for n in range(len(stages[s][0])):
+        total = red_send[s + 1]
+        for n in range(len(stages[s][1])):
             reduce_copy(s, n).wait()
             total = total + red_recv[s, n]
-        red_send[s + 3] = total
-
-    total = red_send[0]
-    for d in range(1, 8):
-        across_copy(d).wait()
-        total = total + a_recv[d - 1]
-    red_send[1] = total
-    for d in range(1, zs):
-        z_copy(d).start()
-
-    @pl.when(middle)
-    def _():
-        for g in range(AHEAD, GROUPS):
-            own_copy(SLOW, g).start()
+        red_send[s + 2] = total
+
+    listing = list_ref[...].astype(F32)
+    code = listing[0] * 64.0 + listing[2] * 8.0 + listing[1]
+    entry = lax.broadcasted_iota(jnp.int32, (1, pairs), 1)
+    code = jnp.where(entry < pairs_ref[0, 0], code, -1.0)
+    code_ref[...] = jnp.broadcast_to(code, (128, pairs)).T
 
     for m in range(3):
         total = None
@@ -304,16 +300,15 @@
             for a in range(2):
                 cross[role, a, m * 256:(m + 1) * 256, :] += total[:, a * 128:(a + 1) * 128]
 
-    total = red_send[1]
-    for d in range(1, zs):
+    total = red_send[0]
+    for d in range(1, 2 * zs):
         z_copy(d).wait()
         total = total + z_recv[d - 1]
-    red_send[2] = total
+    red_send[1] = total
     for g in range(FIRST, AHEAD + FIRST):
         for side in (LEFT, RIGHT):
             when(sides[side][0], lambda side=side, g=g: own_copy(side, g).start())
-    if stages:
-        reduce_start(0)
+    pl.when(inner)(lambda: reduce_start(0))
     cross[0:8] = jnp.zeros((8, 2, 768, 128), F32)
 
     fast_base = (2 - 2 * parity) * 3
@@ -385,16 +380,20 @@
     out_ref[...] = jnp.zeros(out_ref.shape, F32)
 
     def step(g, _):
-        for s in range(len(stages) - 1):
-            @pl.when(g == 7)
+        for s in range(len(stages)):
+            @pl.when((g == 1 + 2 * s) & inner)
             def _(s=s):
                 reduce_end(s)
-                reduce_start(s + 1)
-
-        @pl.when(has_slow & (g < 4) & jnp.logical_not(special))
-        def _():
-            for k in range(2):
-                arrived(SLOW, 2 * g + k)
+                if s + 1 < len(stages):
+                    reduce_start(s + 1)
+                else:
+                    for here, d in ((to_low, -1), (to_high, 1)):
+                        when(here, lambda d=d: total_copy(d).start())
+
+        @pl.when(has_slow & (g == 4) & jnp.logical_not(special))
+        def _():
+            for k in range(GROUPS):
+                arrived(SLOW, k)
 
         for own_side, f_fast, f_slow, next_special, f_early in (
             (LEFT, 0, 2, left_special, 4), (RIGHT, 1, 3, right_special, 5),
@@ -402,10 +401,10 @@
             def service(own_side=own_side, f_fast=f_fast, f_slow=f_slow, next_special=next_special, f_early=f_early):
                 when(g + AHEAD + FIRST < GROUPS, lambda: own_copy(own_side, g + AHEAD + FIRST).start())
                 late = g + AHEAD + FIRST - GROUPS
-                when(has_slow & (late >= 0) & (late < EARLY) & jnp.logical_not(special | next_special),
+                when(has_slow & (late >= 0) & (late < early_here) & jnp.logical_not(special | to_edge[own_side]),
                      lambda: fwd_copy(f_early, late).start())
                 arrived(own_side, g)
-                when(has_slow & ((g >= EARLY) | next_special) & jnp.logical_not(special),
+                when(has_slow & (((g >= early_here) | next_special | edge) & jnp.logical_not(special)),
                      lambda: fwd_copy(f_slow, g).start())
                 fwd_copy(f_fast, g).start()
             when(sides[own_side][0], service)
@@ -445,9 +444,9 @@
                 (jnp.where(g == 5, 4, slow_now_code), jnp.where(g == 5, tile_code[FAST], -5)),
             )
 
-        @pl.when((g == 7) & has_slow & jnp.logical_not(special))
-        def _():
-            accumulate_roles(SLOW_LEFT, 2, 2, True)
+        @pl.when((g >= 6) & has_slow & jnp.logical_not(special))
+        def _():
+            accumulate_roles(SLOW_LEFT, 2, 2 * g - 10, True)
         return 0
 
     lacks = jnp.where(has_left, SLOW_RIGHT, SLOW_LEFT)
@@ -459,15 +458,14 @@
     def pair_step(k, _):
         @pl.when((k == 1) & has_slow & jnp.logical_not(special))
         def _():
-            accumulate_roles(SLOW_LEFT, 2, 4, True)
+            accumulate_roles(SLOW_LEFT, 2, 6, True)
 
         @pl.when((k == 2) & has_slow)
         def _():
             def last_step(n, _):
-                c = (2 * n + 2) % GROUPS
-                accumulate_roles(SLOW_LEFT, 2, c, True)
+                accumulate_roles(SLOW_LEFT, 2, (2 * n + 2) % GROUPS, True)
                 return 0
-            lax.fori_loop(jnp.where(special, 0, 2), 4, last_step, 0)
+            lax.fori_loop(jnp.where(special, 0, 3), 4, last_step, 0)
 
             @pl.when(special)
             def _():
@@ -485,17 +483,17 @@
         )
         return 0
 
-    lax.fori_loop(0, 3, pair_step, 0)
-
-    if stages:
-        reduce_end(len(stages) - 1)
+    lax.fori_loop(0, 2, pair_step, 0)
+    pl.when(outer)(lambda: total_copy(1).wait_recv())
+    for here, d in ((to_low, -1), (to_high, 1)):
+        when(here, lambda d=d: total_copy(d).wait_send())
     for role, here in (
         (FAST, None), (SLOW, has_slow), (FAST_LEFT, has_left), (FAST_RIGHT, has_right),
         (SLOW_LEFT, has_slow & has_left), (SLOW_RIGHT, has_slow & has_right),
     ):
         when(here, lambda role=role: gram_arrived(role))
 
-    summed = red_send[len(stages) + 2]
+    summed = jnp.where(outer, total_ref[...], red_send[len(stages) + 1])
     ridge = summed[0:1, :] / summed[1:2, :] + 1e-06
     upper = gram[:, 0, :] + ridge
     lower = gram[:, 1, :] + ridge
@@ -538,6 +536,8 @@
             + jnp.dot(hot, low, preferred_element_type=F32)
         )
 
+    lax.fori_loop(2, 3, pair_step, 0)
+
     def solve_step(e, _):
         at = pl.ds(pl.multiple_of(e * 32, 32), 32)
         lower, upper, gre, gim = coef_ref[0, at, :], coef_ref[1, at, :], coef_ref[2, at, :], coef_ref[3, at, :]
@@ -568,14 +568,17 @@
             if side == FAST:
                 fwd_copy(f, 0, GROUPS).wait_send()
             else:
-                when(jnp.logical_not(special | next_special),
-                     lambda: fwd_copy(f, EARLY, GROUPS - EARLY).wait_send())
-                when(next_special, lambda: fwd_copy(f, 0, GROUPS).wait_send())
+                for n, here in ((EARLY, jnp.logical_not(middle)), (EARLY_MIDDLE, middle)):
+                    when(here & jnp.logical_not(edge | next_special),
+                         lambda n=n: fwd_copy(f, n, GROUPS - n).wait_send())
+                when((edge | next_special) & jnp.logical_not(special),
+                     lambda: fwd_copy(f, 0, GROUPS).wait_send())
             fwd_gram(f).wait_send()
         when(both(sides[source][0], sides[side][0]), done)
     for f, here, next_special in ((4, has_left, left_special), (5, has_right, right_special)):
-        when(has_slow & here & jnp.logical_not(special | next_special),
-             lambda f=f: fwd_copy(f, 0, EARLY).wait_send())
+        for n, row in ((EARLY, jnp.logical_not(middle)), (EARLY_MIDDLE, middle)):
+            when(has_slow & here & row & jnp.logical_not(special | to_edge[forwards[f][1]]),
+                 lambda f=f, n=n: fwd_copy(f, 0, n).wait_send())
         when(next_special, lambda f=f: fwd_copy(f, 0, GROUPS).wait_send())
 
 
@@ -583,7 +586,7 @@
     pairs = pair_list.shape[-1]
     smem = pl.BlockSpec(memory_space=pltpu.SMEM)
     vmem = pl.BlockSpec(memory_space=pltpu.VMEM)
-    stages = n_lat // 8
+    stages = 2 + n_lat // 8
     zs = n_lon // 2
     dma = pltpu.SemaphoreType.DMA
     solved = pl.pallas_call(
@@ -598,10 +601,10 @@
             pltpu.VMEM((GROUPS, 768, 256), BF16),
             pltpu.VMEM((9, 8, 128), F32),
             pltpu.VMEM((8, 256), F32),
-            pltpu.VMEM((stages + 3, 8, 128), F32),
-            pltpu.VMEM((max(stages, 1), 2, 8, 128), F32),
-            pltpu.VMEM((7, 8, 128), F32),
-            pltpu.VMEM((zs - 1, 8, 128), F32),
+            pltpu.VMEM((stages + 2, 8, 128), F32),
+            pltpu.VMEM((stages, 2, 8, 128), F32),
+            pltpu.VMEM((8, 128), F32),
+            pltpu.VMEM((2 * zs - 1, 8, 128), F32),
             pltpu.VMEM((9, 2, 768, 128), F32),
             pltpu.VMEM((256, 12 * 256), BF16),
             pltpu.VMEM((pairs, 128), F32),
@@ -613,12 +616,11 @@
             dma((8,)),
             dma((4,)),
             dma((4,)),
-            dma((max(stages, 1), 2)),
-            dma((max(stages, 1), 2)),
-            dma((7,)),
-            dma((7,)),
-            dma((zs - 1,)),
-            dma((zs - 1,)),
+            dma((stages, 2)),
+            dma((stages, 2)),
+            dma((2 * zs - 1,)),
+            dma((2 * zs - 1,)),
+            dma,
         ],
         compiler_params=pltpu.CompilerParams(
             collective_id=0, has_side_effects=True, vmem_limit_bytes=56 * 1024 * 1024

time: 62.3 us -> 60.9 us (0.978)
  Pallas kernels: 59.2 us -> 57.6 us
    pallas_call x1, Pallas kernels: 59.2 us -> 57.6 us  [per_device(): pl.pallas_call(functools.partial(kernel, n_lat, n_lon, pairs), out_shape=...]
where the time goes in v3:
time: 60.9 us; the launch traced here: 60.6 us
  Pallas kernels  57.6 us (95%)
  local copies, waits for them, and re-layouts  1.67 us (3%)
  between operations  1.3 us (2%)
    pallas_call x1, Pallas kernels, per_device(): pl.pallas_call(functools.partial(kernel, n_lat, n_lon, pairs), out_shape=...  57.6 us
    unnamed x1, local copies, waits for them, and re-layouts  1.67 us

profile of v3, /device:TPU:4, one launch (start us, length us, event | category | flops | bytes accessed | tf_op | source)
XLA Modules:
  0.0 60.6 jit_solution(13249216145123509014)
XLA Ops:
  1.3 57.6 %shard_map.64 = f32[12,256,256]{2,1,0:T(8,128)S(1)} custom-call(s32[1,1]{1,0:T(1,128)S(6)} %copy.9.count_ref, s32[1,1]{1,0:T(1,128)S(6)} %copy.10.pairs_ref, s32[16]{0:T(128)} %bins_ref.1, s32[3,1,256]{2,1,0:T(1,128)} %bitcast.7, bf16[128,128]{1,0:T(8,128)(2,1)} %constant.2.clone.dft_ref, bf16[3,64,128,128]{3,2,1,0:T(8,128)(2,1)} %bitcast.6), custom_call_target="tpu_custom_call" | custom-call | tf_op jit(solution)/shard_map/pallas_call | solution.py:592
  58.9 1.7 %copy.8 = f32[1,1,256,12,256]{4,2,3,1,0:T(8,128)} copy(f32[1,1,256,12,256]{4,2,3,1,0:T(8,128)S(1)} %bitcast.5) | data formatting | bytes 6291456

commit v4 on v3

--- a/solution.py
+++ b/solution.py
@@ -152,7 +152,6 @@
         has_slow.astype(jnp.int32) + has_left.astype(jnp.int32) + has_right.astype(jnp.int32)
         + (1 + len(rings))
     )
-    pl.semaphore_wait(barrier, greeted)
 
     def remote(src, dst, send, recv, device):
         return pltpu.make_async_remote_copy(
@@ -166,7 +165,13 @@
             near_recv.at[lands[side], g], sides[side][1],
         )
 
-    def spectra_step(g, _):
+    def send_own(g):
+        when(has_slow, lambda: own_copy(SLOW, g).start())
+        own_copy(FAST, g).start()
+        for side in (LEFT, RIGHT):
+            when(sides[side][0] & (g < FIRST), lambda side=side: own_copy(side, g).start())
+
+    def spectra_step(g, first=False):
         series_copy(g).wait()
         total = None
         for j in range(4):
@@ -179,17 +184,21 @@
         masked = jnp.where(live[None], total.reshape(3, SLOTS, 256), 0.0)
         spec = masked.reshape(3 * SLOTS, 256).astype(BF16)
         lhs[g, 0:384, :] = spec
-        when(has_slow, lambda: own_copy(SLOW, g).start())
-        own_copy(FAST, g).start()
-        for side in (LEFT, RIGHT):
-            when(sides[side][0] & (g < FIRST), lambda side=side: own_copy(side, g).start())
+        if first:
+            pl.semaphore_wait(barrier, greeted)
+        send_own(g)
         lhs[g, 384:768, 0:128] = spec[:, 128:256]
         lhs[g, 384:768, 128:256] = -spec[:, 0:128]
         wide = spec[0:256].astype(F32)
         power_ref[...] += jnp.sum((wide * wide).reshape(32, 8, 256), axis=0)
+
+    spectra_step(0, True)
+
+    def later_spectra(g, _):
+        spectra_step(g)
         return 0
 
-    lax.fori_loop(0, GROUPS, spectra_step, 0)
+    lax.fori_loop(1, GROUPS, later_spectra, 0)
 
     srow = lax.broadcasted_iota(jnp.int32, (8, 128), 0)
     power = 0.5 * jnp.sum(power_ref[...], keepdims=True)

time: 60.9 us -> 60.5 us (level)
  no operation moved by 1% of the time
where the time goes in v4:
time: 60.5 us; the launch traced here: 60.2 us
  Pallas kernels  57.2 us (95%)
  local copies, waits for them, and re-layouts  1.67 us (3%)
  between operations  1.3 us (2%)
    pallas_call x1, Pallas kernels, per_device(): pl.pallas_call(functools.partial(kernel, n_lat, n_lon, pairs), out_shape=...  57.2 us
    unnamed x1, local copies, waits for them, and re-layouts  1.67 us

profile of v4, /device:TPU:4, one launch (start us, length us, event | category | flops | bytes accessed | tf_op | source)
XLA Modules:
  0.0 60.2 jit_solution(5183359595265090600)
XLA Ops:
  1.3 57.2 %shard_map.64 = f32[12,256,256]{2,1,0:T(8,128)S(1)} custom-call(s32[1,1]{1,0:T(1,128)S(6)} %copy.9.count_ref, s32[1,1]{1,0:T(1,128)S(6)} %copy.10.pairs_ref, s32[16]{0:T(128)} %bins_ref.1, s32[3,1,256]{2,1,0:T(1,128)} %bitcast.7, bf16[128,128]{1,0:T(8,128)(2,1)} %constant.2.clone.dft_ref, bf16[3,64,128,128]{3,2,1,0:T(8,128)(2,1)} %bitcast.6), custom_call_target="tpu_custom_call" | custom-call | tf_op jit(solution)/shard_map/pallas_call | solution.py:601
  58.5 1.7 %copy.8 = f32[1,1,256,12,256]{4,2,3,1,0:T(8,128)} copy(f32[1,1,256,12,256]{4,2,3,1,0:T(8,128)S(1)} %bitcast.5) | data formatting | bytes 6291456
